TPU v7x, 32 devices: a whole 2x2x4 slice. The times are simulated.
32 devices in a mesh: rep: 16 (over z, y, x), fsdp: 2 (over core).
Axes of the slice: x: 2, y: 2, z: 4, core: 2. Of those that a mesh axis runs over, the one named last changes fastest.
Arguments:
- tokens: bfloat16 [32, 1024, 768], P('rep', 'fsdp'), may hold values from -6 to 6
- lengths: int32 [32, 8], P('rep'), may hold values from 1 to 1017, as said below
- w_qkv: bfloat16 [768, 2304], P('fsdp'), may hold values from -0.21875 to 0.21875
- w_out: bfloat16 [768, 768], P('fsdp'), may hold values from -1.75 to 1.75
- w_gate: bfloat16 [768, 3072], P('fsdp'), may hold values from -0.21875 to 0.21875
- w_up: bfloat16 [768, 3072], P('fsdp'), may hold values from -0.21875 to 0.21875
- w_down: bfloat16 [3072, 768], P('fsdp'), may hold values from -0.109375 to 0.109375
- norm1_gain: bfloat16 [768], P('fsdp'), may hold values from 0.5 to 1.5
- norm1_bias: bfloat16 [768], P('fsdp'), may hold values from -2 to 2
- norm2_gain: bfloat16 [768], P('fsdp'), may hold values from 0.5 to 1.5
- norm2_bias: bfloat16 [768], P('fsdp'), may hold values from -2 to 2
- cotangent: bfloat16 [32, 1024, 768], P('rep', 'fsdp'), may hold values from -6 to 6
Outputs:
- activations: bfloat16 [32, 1024, 768], P('rep', 'fsdp')
- input_grad: float32 [32, 1024, 768], P('rep', 'fsdp')
- qkv_grad: float32 [768, 2304], P('fsdp')
- out_grad: float32 [768, 768], P('fsdp')
- gate_grad: float32 [768, 3072], P('fsdp')
- up_grad: float32 [768, 3072], P('fsdp')
- down_grad: float32 [3072, 768], P('fsdp')
- gain_one_grad: float32 [768], P('fsdp')
- bias_one_grad: float32 [768], P('fsdp')
- gain_two_grad: float32 [768], P('fsdp')
- bias_two_grad: float32 [768], P('fsdp')
Inputs may be any that keep to these rules, and one draw needn't show every extreme that they name: Each row of 8 lengths sums to 1024; in each row the document that holds position 512 begins before position 256 and ends after position 768.
All inputs are finite; a program needn't handle non-finite values.
Results may differ from a plain program's by a relative error of at most 0.014.
Values may be sent and summed in bfloat16 or wider, within the bound.
A program may use at most 256 MiB of HBM per device.

v0:
```python
import jax
import jax.numpy as jnp
from jax import lax
from jax.sharding import PartitionSpec as P

HEADS = 12
HEAD_DIM = 64


EPSILON = 1e-05


def doc_tables(doc_lengths, seq_len):
    doc_ends = jnp.cumsum(doc_lengths)
    doc_starts = doc_ends - doc_lengths
    places = jnp.arange(seq_len, dtype=jnp.int32)
    segment = jnp.sum((places[:, None] >= doc_ends[None, :]).astype(jnp.int32), axis=1)
    member = segment[:, None] == jnp.arange(doc_lengths.shape[0], dtype=jnp.int32)[None, :]
    begins = jnp.sum(jnp.where(member, doc_starts[None, :], 0), axis=1)
    return (segment, places - begins)


def rope_tables(positions):
    half_dim = HEAD_DIM // 2
    frequencies = 1000.0 ** (-2.0 * jnp.arange(half_dim, dtype=jnp.float32) / HEAD_DIM)
    angles = positions.astype(jnp.float32)[:, None] * frequencies[None, :]
    return (jnp.cos(angles), jnp.sin(angles))


def rotate(values, cosine_table, sine_table):
    row_count = values.shape[0]
    split_heads = values.reshape(row_count, HEADS, HEAD_DIM)
    first_half = split_heads[..., : HEAD_DIM // 2]
    second_half = split_heads[..., HEAD_DIM // 2 :]
    cosine_rows = cosine_table[:, None, :]
    sine_rows = sine_table[:, None, :]
    turned = jnp.concatenate(
        [
            first_half * cosine_rows - second_half * sine_rows,
            second_half * cosine_rows + first_half * sine_rows,
        ],
        axis=-1,
    )
    return turned.reshape(row_count, HEADS * HEAD_DIM)


def norm_forward(values, gain_vec, bias_vec):
    centre = values - jnp.mean(values, axis=-1, keepdims=True)
    inv_std = lax.rsqrt(jnp.mean(centre * centre, axis=-1, keepdims=True) + EPSILON)
    unit_rows = centre * inv_std
    return (unit_rows * gain_vec + bias_vec, unit_rows, inv_std)


def norm_back(grad_norm, unit_rows, inv_std):
    return inv_std * (
        grad_norm
        - jnp.mean(grad_norm, axis=-1, keepdims=True)
        - unit_rows * jnp.mean(grad_norm * unit_rows, axis=-1, keepdims=True)
    )


def heads_of(values):
    return values.reshape(values.shape[0], HEADS, HEAD_DIM)


def product(left_side, right_side):
    return jnp.dot(left_side, right_side, preferred_element_type=jnp.float32)


def product_left_t(left_side, right_side):
    return lax.dot_general(
        left_side, right_side, (((0,), (0,)), ((), ())), preferred_element_type=jnp.float32
    )


def product_right_t(left_side, right_side):
    return lax.dot_general(
        left_side, right_side, (((1,), (1,)), ((), ())), preferred_element_type=jnp.float32
    )


def masked_scores(query_heads, key_heads, same_doc, score_scale):
    raw_scores = jnp.einsum(
        "qhd,khd->hqk", query_heads, key_heads, preferred_element_type=jnp.float32
    )
    return jnp.where(same_doc[None], raw_scores * score_scale, -1e30)


def shards(
    tokens,
    lengths,
    w_qkv,
    w_out,
    w_gate,
    w_up,
    w_down,
    norm1_gain,
    norm1_bias,
    norm2_gain,
    norm2_bias,
    cotangent,
):
    micro_count = tokens.shape[0]
    tok_mb = tokens.shape[1]
    model_width = tokens.shape[2]
    seq_len = tok_mb * lax.axis_size("fsdp")
    offset = lax.axis_index("fsdp") * tok_mb
    score_scale = HEAD_DIM ** (-0.5)
    totals = None
    outputs = []
    input_grads = []
    for micro_idx in range(micro_count):
        gathered = (
            lax.all_gather(w_qkv, "fsdp", axis=0, tiled=True),
            lax.all_gather(w_out, "fsdp", axis=0, tiled=True),
            lax.all_gather(w_gate, "fsdp", axis=0, tiled=True),
            lax.all_gather(w_up, "fsdp", axis=0, tiled=True),
            lax.all_gather(w_down, "fsdp", axis=0, tiled=True),
            lax.all_gather(norm1_gain, "fsdp", axis=0, tiled=True),
            lax.all_gather(norm1_bias, "fsdp", axis=0, tiled=True),
            lax.all_gather(norm2_gain, "fsdp", axis=0, tiled=True),
            lax.all_gather(norm2_bias, "fsdp", axis=0, tiled=True),
        )
        stream = tokens[micro_idx]
        stream_wide = stream.astype(jnp.float32)
        segment_all, positions_all = doc_tables(lengths[micro_idx], seq_len)
        segment_own = lax.dynamic_slice_in_dim(segment_all, offset, tok_mb)
        positions_own = lax.dynamic_slice_in_dim(positions_all, offset, tok_mb)
        cosine_table, sine_table = rope_tables(positions_own)
        projected = product(stream, gathered[0])
        queries = rotate(projected[:, :model_width], cosine_table, sine_table).astype(jnp.bfloat16)
        key_own = rotate(
            projected[:, model_width : 2 * model_width], cosine_table, sine_table
        ).astype(jnp.bfloat16)
        value_own = projected[:, 2 * model_width :].astype(jnp.bfloat16)
        key_rows, value_rows = (
            lax.all_gather(key_own, "fsdp", axis=0, tiled=True),
            lax.all_gather(value_own, "fsdp", axis=0, tiled=True),
        )
        same_doc = segment_own[:, None] == segment_all[None, :]
        scores = masked_scores(heads_of(queries), heads_of(key_rows), same_doc, score_scale)
        row_max = jnp.max(scores, axis=-1, keepdims=True)
        exp_scores = jnp.exp(scores - row_max)
        row_total = jnp.sum(exp_scores, axis=-1, keepdims=True)
        log_total = row_max + jnp.log(row_total)
        attn_low = (exp_scores / row_total).astype(jnp.bfloat16)
        context = jnp.einsum(
            "hqk,khd->qhd", attn_low, heads_of(value_rows), preferred_element_type=jnp.float32
        )
        context = context.reshape(tok_mb, model_width).astype(jnp.bfloat16)
        first_sum = stream_wide + product(context, gathered[1])
        normed, unit_one, inv_one = norm_forward(
            first_sum, gathered[5].astype(jnp.float32), gathered[6].astype(jnp.float32)
        )
        normed_low = normed.astype(jnp.bfloat16)
        gate_act = product(normed_low, gathered[2])
        up_act = product(normed_low, gathered[3])
        gate_sig = jax.nn.sigmoid(gate_act)
        gate_silu = gate_act * gate_sig
        hidden = (gate_silu * up_act).astype(jnp.bfloat16)
        second_sum = normed + product(hidden, gathered[4])
        result, unit_two, inv_two = norm_forward(
            second_sum, gathered[7].astype(jnp.float32), gathered[8].astype(jnp.float32)
        )
        outputs.append(result.astype(jnp.bfloat16))
        back_weights = (
            lax.all_gather(w_qkv, "fsdp", axis=0, tiled=True),
            lax.all_gather(w_out, "fsdp", axis=0, tiled=True),
            lax.all_gather(w_gate, "fsdp", axis=0, tiled=True),
            lax.all_gather(w_up, "fsdp", axis=0, tiled=True),
            lax.all_gather(w_down, "fsdp", axis=0, tiled=True),
            lax.all_gather(norm1_gain, "fsdp", axis=0, tiled=True),
            lax.all_gather(norm1_bias, "fsdp", axis=0, tiled=True),
            lax.all_gather(norm2_gain, "fsdp", axis=0, tiled=True),
            lax.all_gather(norm2_bias, "fsdp", axis=0, tiled=True),
        )
        grad_out = cotangent[micro_idx].astype(jnp.float32)
        bias_two_grad = jnp.sum(grad_out, axis=0)
        gain_two_grad = jnp.sum(grad_out * unit_two, axis=0)
        grad_second = norm_back(grad_out * back_weights[7].astype(jnp.float32), unit_two, inv_two)
        grad_mixed = grad_second.astype(jnp.bfloat16)
        down_grad = product_left_t(hidden, grad_mixed)
        grad_hidden = product_right_t(grad_mixed, back_weights[4])
        grad_gate_act = (
            grad_hidden * up_act * gate_sig * (1.0 + gate_act * (1.0 - gate_sig))
        ).astype(jnp.bfloat16)
        grad_up_act = (grad_hidden * gate_silu).astype(jnp.bfloat16)
        gate_grad = product_left_t(normed_low, grad_gate_act)
        up_grad = product_left_t(normed_low, grad_up_act)
        grad_normed = (
            grad_second
            + product_right_t(grad_gate_act, back_weights[2])
            + product_right_t(grad_up_act, back_weights[3])
        )
        bias_one_grad = jnp.sum(grad_normed, axis=0)
        gain_one_grad = jnp.sum(grad_normed * unit_one, axis=0)
        grad_first = norm_back(grad_normed * back_weights[5].astype(jnp.float32), unit_one, inv_one)
        grad_attended = grad_first.astype(jnp.bfloat16)
        out_grad = product_left_t(context, grad_attended)
        grad_context = product_right_t(grad_attended, back_weights[1]).astype(jnp.bfloat16)
        scores_again = masked_scores(heads_of(queries), heads_of(key_rows), same_doc, score_scale)
        attn_probs = jnp.exp(scores_again - log_total)
        context_heads = heads_of(grad_context)
        grad_probs = jnp.einsum(
            "qhd,khd->hqk", context_heads, heads_of(value_rows), preferred_element_type=jnp.float32
        )
        grad_scores = (
            score_scale
            * attn_probs
            * (grad_probs - jnp.sum(attn_probs * grad_probs, axis=-1, keepdims=True))
        ).astype(jnp.bfloat16)
        grad_queries = jnp.einsum(
            "hqk,khd->qhd", grad_scores, heads_of(key_rows), preferred_element_type=jnp.float32
        ).reshape(tok_mb, model_width)
        grad_keys_all = jnp.einsum(
            "hqk,qhd->khd", grad_scores, heads_of(queries), preferred_element_type=jnp.float32
        ).reshape(seq_len, model_width)
        grad_values_all = jnp.einsum(
            "hqk,qhd->khd",
            attn_probs.astype(jnp.bfloat16),
            context_heads,
            preferred_element_type=jnp.float32,
        ).reshape(seq_len, model_width)
        grad_keys, grad_values = (
            lax.psum_scatter(grad_keys_all, "fsdp", scatter_dimension=0, tiled=True),
            lax.psum_scatter(grad_values_all, "fsdp", scatter_dimension=0, tiled=True),
        )
        grad_projected = jnp.concatenate(
            [
                rotate(grad_queries, cosine_table, -sine_table),
                rotate(grad_keys, cosine_table, -sine_table),
                grad_values,
            ],
            axis=1,
        ).astype(jnp.bfloat16)
        qkv_grad = product_left_t(stream, grad_projected)
        input_grads.append(grad_first + product_right_t(grad_projected, back_weights[0]))
        terms = (
            qkv_grad,
            out_grad,
            gate_grad,
            up_grad,
            down_grad,
            gain_one_grad,
            bias_one_grad,
            gain_two_grad,
            bias_two_grad,
        )
        totals = (
            terms if totals is None else tuple((total + term for total, term in zip(totals, terms)))
        )
    reduced = (
        lax.psum_scatter(totals[0], "fsdp", scatter_dimension=0, tiled=True),
        lax.psum_scatter(totals[1], "fsdp", scatter_dimension=0, tiled=True),
        lax.psum_scatter(totals[2], "fsdp", scatter_dimension=0, tiled=True),
        lax.psum_scatter(totals[3], "fsdp", scatter_dimension=0, tiled=True),
        lax.psum_scatter(totals[4], "fsdp", scatter_dimension=0, tiled=True),
        lax.psum_scatter(totals[5], "fsdp", scatter_dimension=0, tiled=True),
        lax.psum_scatter(totals[6], "fsdp", scatter_dimension=0, tiled=True),
        lax.psum_scatter(totals[7], "fsdp", scatter_dimension=0, tiled=True),
        lax.psum_scatter(totals[8], "fsdp", scatter_dimension=0, tiled=True),
    )
    summed = lax.psum(
        (
            reduced[0],
            reduced[1],
            reduced[2],
            reduced[3],
            reduced[4],
            reduced[5],
            reduced[6],
            reduced[7],
            reduced[8],
        ),
        "rep",
    )
    return (
        jnp.stack(outputs),
        jnp.stack(input_grads),
        summed[0],
        summed[1],
        summed[2],
        summed[3],
        summed[4],
        summed[5],
        summed[6],
        summed[7],
        summed[8],
    )


def solution(mesh):
    placed = (
        P("rep", "fsdp", None),
        P("rep", None),
        P("fsdp", None),
        P("fsdp", None),
        P("fsdp", None),
        P("fsdp", None),
        P("fsdp", None),
        P("fsdp"),
        P("fsdp"),
        P("fsdp"),
        P("fsdp"),
        P("rep", "fsdp", None),
    )
    return jax.shard_map(
        shards,
        mesh=mesh,
        in_specs=placed,
        out_specs=(
            P("rep", "fsdp", None),
            P("rep", "fsdp", None),
            P("fsdp", None),
            P("fsdp", None),
            P("fsdp", None),
            P("fsdp", None),
            P("fsdp", None),
            P("fsdp"),
            P("fsdp"),
            P("fsdp"),
            P("fsdp"),
        ),
        check_vma=False,
    )
```

profile of v0, /device:TPU:0, one launch (start us, length us, event | category | flops | bytes accessed | tf_op | source)
XLA Modules:
  0.0 1012.3 jit_solution(17108315390430391156)
XLA Ops:
  11.5 13.5 %all-gather.14.cloned.1.call-done = bf16[768,2304]{1,0:T(8,128)(2,1)} async-done(((bf16[384,2304]{1,0:T(8,128)(2,1)}), bf16[768,2304]{1,0:T(8,128)(2,1)}) %all-gather.14.cloned.1.call-update) | async-done | bytes 3538960 | tf_op jit(solution)/shard_map/all_gather | solution.py:114
  67.2 12.3 %fusion.12 = (f32[12,512]{1,0:T(8,128)S(1)}, f32[12,512,1024]{2,1,0:T(8,128)}) fusion(pred[512,1024]{1,0:T(8,128)(4,1)S(1)} %broadcast_compare_fusion.1, bf16[1024,12,64]{0,2,1:T(8,128)(2,1)} %bitcast.213, bf16[512,12,32]{0,2,1:T(8,128)(2,1)S(1)} %copy-done.28, bf16[512,12,32]{0,2,1:T(8,128)(2,1)S(1)} %get-tuple-element.102), kind=kOutput, calls=%fused_computation.22 | convolution fusion | flops 825747456 | bytes 28073984 | tf_op jit(solution)/shard_map/qhd,khd->hqk/dot_general | solution.py:83
  79.5 12.4 %fusion = f32[12,512]{1,0:T(8,128)S(1)} fusion(f32[12,512]{1,0:T(8,128)S(1)} %get-tuple-element.136, f32[12,512,1024]{2,1,0:T(8,128)} %get-tuple-element.137, pred[512,1024]{1,0:T(8,128)(4,1)S(1)} %broadcast_compare_fusion.1), kind=kLoop, calls=%fused_computation.12 | loop fusion | flops 25159680 | bytes 25739264 | tf_op jit(solution)/shard_map/reduce_sum | solution.py:144
  93.7 13.6 %fusion.35 = bf16[12,64,512]{2,1,0:T(8,128)(2,1)} fusion(bf16[1024,12,64]{0,2,1:T(8,128)(2,1)S(1)} %bitcast.205, f32[12,512]{1,0:T(8,128)S(1)} %fusion, f32[12,512]{1,0:T(8,128)S(1)} %copy-done.64, f32[12,512,1024]{2,1,0:T(8,128)} %get-tuple-element.137, pred[512,1024]{1,0:T(8,128)(4,1)S(1)} %broadcast_compare_fusion.1), kind=kOutput, calls=%fused_computation.98 | convolution fusion | flops 837156864 | bytes 28098560 | tf_op jit(solution)/shard_map/hqk,khd->qhd/dot_general | solution.py:147
  107.4 12.9 %fusion.13 = (f32[12,512]{1,0:T(8,128)S(1)}, f32[12,512,1024]{2,1,0:T(8,128)}) fusion(pred[512,1024]{1,0:T(8,128)(4,1)S(1)} %broadcast_compare_fusion, bf16[1024,12,64]{0,2,1:T(8,128)(2,1)} %bitcast.215, bf16[512,12,32]{0,2,1:T(8,128)(2,1)S(1)} %copy-done.32, bf16[512,12,32]{0,2,1:T(8,128)(2,1)S(1)} %copy-done.30), kind=kOutput, calls=%fused_computation.23 | convolution fusion | flops 825747456 | bytes 28073984 | tf_op jit(solution)/shard_map/qhd,khd->hqk/dot_general | solution.py:83
  120.3 13.3 %fusion.1 = f32[12,512]{1,0:T(8,128)S(1)} fusion(f32[12,512]{1,0:T(8,128)S(1)} %get-tuple-element.140, f32[12,512,1024]{2,1,0:T(8,128)} %get-tuple-element.141, pred[512,1024]{1,0:T(8,128)(4,1)S(1)} %broadcast_compare_fusion), kind=kLoop, calls=%fused_computation.13 | loop fusion | flops 25159680 | bytes 25739264 | tf_op jit(solution)/shard_map/reduce_sum | solution.py:144
  135.4 14.7 %fusion.34 = bf16[12,64,512]{2,1,0:T(8,128)(2,1)} fusion(bf16[1024,12,64]{0,2,1:T(8,128)(2,1)S(1)} %bitcast.203, f32[12,512]{1,0:T(8,128)S(1)} %fusion.1, f32[12,512]{1,0:T(8,128)S(1)} %get-tuple-element.140, f32[12,512,1024]{2,1,0:T(8,128)} %get-tuple-element.141, pred[512,1024]{1,0:T(8,128)(4,1)S(1)} %broadcast_compare_fusion), kind=kOutput, calls=%fused_computation.97 | convolution fusion | flops 837156864 | bytes 28098560 | tf_op jit(solution)/shard_map/hqk,khd->qhd/dot_general | solution.py:147
  155.7 7.1 fusion.98
  162.8 9.0 multiply_convert_fusion.6
  194.1 9.7 multiply_convert_fusion.4
  208.7 7.6 multiply_reduce_fusion.3
  216.4 9.9 multiply_convert_fusion.2
  231.2 7.6 multiply_reduce_fusion.2
  243.7 13.1 %fusion.4 = f32[12,64,1024]{2,1,0:T(8,128)} fusion(bf16[512,12,64]{0,2,1:T(8,128)(2,1)S(1)} %bitcast.229, f32[12,512]{1,0:T(8,128)S(1)} %log_add_fusion, f32[12,512,1024]{2,1,0:T(8,128)} %get-tuple-element.141, pred[512,1024]{1,0:T(8,128)(4,1)S(1)} %copy-done.4), kind=kOutput, calls=%fused_computation.16 | convolution fusion | flops 830472192 | bytes 29646848 | tf_op jit(solution)/shard_map/hqk,qhd->khd/dot_general | solution.py:218
  262.7 15.1 %fusion.6 = f32[12,64,1024]{2,1,0:T(8,128)} fusion(bf16[512,12,64]{0,2,1:T(8,128)(2,1)} %bitcast.231, f32[12,512]{1,0:T(8,128)S(1)} %log_add_fusion.1, f32[12,512,1024]{2,1,0:T(8,128)} %get-tuple-element.137, pred[512,1024]{1,0:T(8,128)(4,1)S(1)} %copy-done.6), kind=kOutput, calls=%fused_computation.17 | convolution fusion | flops 830472192 | bytes 29646848 | tf_op jit(solution)/shard_map/hqk,qhd->khd/dot_general | solution.py:218
  277.9 18.7 %multiply_reduce_fusion.1 = (f32[12,512]{1,0:T(8,128)S(1)}, f32[12,512,1024]{2,1,0:T(8,128)}) fusion(f32[12,512]{1,0:T(8,128)S(1)} %log_add_fusion.1, f32[12,512,1024]{2,1,0:T(8,128)} %get-tuple-element.137, pred[512,1024]{1,0:T(8,128)(4,1)S(1)} %copy-done.6, bf16[512,12,64]{0,2,1:T(8,128)(2,1)} %bitcast.232, bf16[1024,12,64]{0,2,1:T(8,128)(2,1)} %bitcast.206), kind=kOutput, calls=%fused_computation.4 | convolution fusion | flops 836757504 | bytes 53264384 | tf_op jit(solution)/shard_map/qhd,khd->hqk/dot_general | solution.py:204
  296.6 17.3 %multiply_convert_fusion.1 = bf16[12,512,1024]{2,1,0:T(8,128)(2,1)S(1)} fusion(f32[12,512,1024]{2,1,0:T(8,128)} %get-tuple-element.157, f32[12,512]{1,0:T(8,128)S(1)} %get-tuple-element.156, f32[12,512]{1,0:T(8,128)S(1)} %log_add_fusion.1, f32[12,512,1024]{2,1,0:T(8,128)} %get-tuple-element.137, pred[512,1024]{1,0:T(8,128)(4,1)S(1)} %copy-done.6), kind=kLoop, calls=%fused_computation.3 | loop fusion | flops 44040192 | bytes 63488000 | tf_op jit(solution)/shard_map/convert_element_type | solution.py:211
  319.5 20.6 %multiply_reduce_fusion = (f32[12,512]{1,0:T(8,128)S(1)}, f32[12,512,1024]{2,1,0:T(8,128)}) fusion(f32[12,512]{1,0:T(8,128)S(1)} %log_add_fusion, f32[12,512,1024]{2,1,0:T(8,128)} %get-tuple-element.141, pred[512,1024]{1,0:T(8,128)(4,1)S(1)} %copy-done.4, bf16[512,12,64]{0,2,1:T(8,128)(2,1)S(1)} %bitcast.230, bf16[1024,12,64]{0,2,1:T(8,128)(2,1)} %bitcast.204), kind=kOutput, calls=%fused_computation.1 | convolution fusion | flops 836757504 | bytes 53264384 | tf_op jit(solution)/shard_map/qhd,khd->hqk/dot_general | solution.py:204
  340.1 17.3 %multiply_convert_fusion = bf16[12,512,1024]{2,1,0:T(8,128)(2,1)S(1)} fusion(f32[12,512,1024]{2,1,0:T(8,128)} %get-tuple-element.155, f32[12,512]{1,0:T(8,128)S(1)} %get-tuple-element.154, f32[12,512]{1,0:T(8,128)S(1)} %log_add_fusion, f32[12,512,1024]{2,1,0:T(8,128)} %get-tuple-element.141, pred[512,1024]{1,0:T(8,128)(4,1)S(1)} %copy-done.4), kind=kLoop, calls=%fused_computation | loop fusion | flops 44040192 | bytes 63488000 | tf_op jit(solution)/shard_map/convert_element_type | solution.py:211
  407.9 10.0 convolution_bitcast_fusion.1
  417.9 10.8 %convolution_bitcast_fusion = f32[512,12,64]{0,2,1:T(8,128)S(1)} fusion(bf16[1024,12,64]{0,2,1:T(8,128)(2,1)S(1)} %bitcast.216, bf16[12,512,1024]{2,1,0:T(8,128)(2,1)} %copy-done.1), kind=kOutput, calls=%fused_computation.87 | convolution fusion | flops 805306368 | bytes 15728640 | tf_op jit(solution)/shard_map/hqk,khd->qhd/dot_general | solution.py:212
  452.3 19.0 %reduce-scatter.18.cloned.1.call-done = f32[384,2304]{0,1:T(8,128)} async-done(((f32[768,2304]{0,1:T(8,128)}), f32[384,2304]{0,1:T(8,128)}) %reduce-scatter.18.cloned.1.call-update) | async-done | bytes 3538960 | tf_op jit(solution)/shard_map/reduce_scatter | solution.py:253
  477.5 45.6 %all-reduce.4 = (f32[384]{0:T(512)}, f32[384]{0:T(512)}, f32[384]{0:T(512)}, f32[384]{0:T(512)}) all-reduce(f32[384]{0:T(512)S(1)} %dynamic-slice.1, f32[384]{0:T(512)S(1)} %dynamic-slice.3, f32[384]{0:T(512)S(1)} %dynamic-slice.5, f32[384]{0:T(512)S(1)} %dynamic-slice.7), channel_id=1, replica_groups=mesh['rep'=16,'fsdp'=2] {'rep'}, use_global_device_ids=true, to_apply=%region_45.46 | all-reduce | flops 1536 | bytes 12288 | tf_op jit(solution)/shard_map/psum | solution.py:263
  534.2 455.0 %all-reduce.9.cloned.1.call-done = (f32[384,2304]{0,1:T(8,128)}, f32[384,768]{1,0:T(8,128)}, f32[384,3072]{1,0:T(8,128)}, f32[384,3072]{1,0:T(8,128)}, f32[1536,768]{1,0:T(8,128)}) async-done(((f32[384,2304]{0,1:T(8,128)}, f32[384,768]{1,0:T(8,128)}, f32[384,3072]{1,0:T(8,128)}, f32[384,3072]{1,0:T(8,128)}, f32[1536,768]{1,0:T(8,128)}), (f32[384,2304]{0,1:T(8,128)}, f32[384,768]{1,0:T(8,128)}, ...) | async-done | bytes 18874384 | tf_op jit(solution)/shard_map/psum | solution.py:263
  (409 shorter events, 209.6 us)
Async XLA Ops:
  7.2 17.8 %all-gather.14.cloned.1.call-start = ((), (), s32[]{:S(2)}) async-start(), calls=%async_computation.9 | async-start | bytes 5308416 | tf_op jit(solution)/shard_map/all_gather | solution.py:114
  7.9 59.3 %all-gather.18.cloned.1.call-start = ((), (), s32[]{:S(2)}) async-start(), calls=%async_computation.11 | async-start | bytes 2359296 | tf_op jit(solution)/shard_map/all_gather | solution.py:137
  37.4 54.5 %all-gather.16.cloned.1.call-start = ((), (), s32[]{:S(2)}) async-start(), calls=%async_computation.10 | async-start | bytes 2359296 | tf_op jit(solution)/shard_map/all_gather | solution.py:138
  39.9 67.5 %all-gather.30.cloned.1.call-start = ((), (), s32[]{:S(2)}) async-start(), calls=%async_computation.17 | async-start | bytes 2359296 | tf_op jit(solution)/shard_map/all_gather | solution.py:137
  52.2 81.4 %all-gather.28.cloned.1.call-start = ((), (), s32[]{:S(2)}) async-start(), calls=%async_computation.16 | async-start | bytes 2359296 | tf_op jit(solution)/shard_map/all_gather | solution.py:138
  54.7 95.4 %all-gather.20.cloned.1.call-start = ((), (), s32[]{:S(2)}) async-start(), calls=%async_computation.12 | async-start | bytes 1769472 | tf_op jit(solution)/shard_map/all_gather | solution.py:115
  55.3 100.4 %all-gather.22.cloned.1.call-start = ((), (), s32[]{:S(2)}) async-start(), calls=%async_computation.13 | async-start | bytes 7077888 | tf_op jit(solution)/shard_map/all_gather | solution.py:116
  56.1 106.7 %all-gather.24.cloned.1.call-start = ((), (), s32[]{:S(2)}) async-start(), calls=%async_computation.14 | async-start | bytes 7077888 | tf_op jit(solution)/shard_map/all_gather | solution.py:117
  56.8 115.0 %all-gather.26.cloned.1.call-start = ((), (), s32[]{:S(2)}) async-start(), calls=%async_computation.15 | async-start | bytes 7077888 | tf_op jit(solution)/shard_map/all_gather | solution.py:118
  57.5 371.2 %reduce-scatter.16.cloned.1.call-start = ((), (), s32[]{:S(2)}) async-start(), calls=%async_computation.21 | async-start | bytes 4718592 | tf_op jit(solution)/shard_map/reduce_scatter | solution.py:226
  61.4 110.4 %copy-start.76 = (f32[768]{0:T(1024)}, f32[768]{0:T(1024)S(1)}, u32[]{:S(2)}) copy-start(f32[768]{0:T(1024)S(1)} %reshape.462) | copy-start | bytes 9220
  66.8 68.5 %copy-start.3 = (pred[512,1024]{1,0:T(8,128)(4,1)}, pred[512,1024]{1,0:T(8,128)(4,1)S(1)}, u32[]{:S(2)}) copy-start(pred[512,1024]{1,0:T(8,128)(4,1)S(1)} %broadcast_compare_fusion) | copy-start | bytes 1572868
  256.8 174.5 %reduce-scatter.12.cloned.1.call-start = ((), (), s32[]{:S(2)}) async-start(), calls=%async_computation.19 | async-start | bytes 4718592 | tf_op jit(solution)/shard_map/reduce_scatter | solution.py:226
  277.8 155.8 %reduce-scatter.10.cloned.1.call-start = ((), (), s32[]{:S(2)}) async-start(), calls=%async_computation.18 | async-start | bytes 4718592 | tf_op jit(solution)/shard_map/reduce_scatter | solution.py:225
  319.4 118.5 %reduce-scatter.14.cloned.1.call-start = ((), (), s32[]{:S(2)}) async-start(), calls=%async_computation.20 | async-start | bytes 4718592 | tf_op jit(solution)/shard_map/reduce_scatter | solution.py:225
  363.0 87.6 %reduce-scatter.20.cloned.1.call-start = ((), (), s32[]{:S(2)}) async-start(), calls=%async_computation.23 | async-start | bytes 3538944 | tf_op jit(solution)/shard_map/reduce_scatter | solution.py:254
  367.9 82.7 %reduce-scatter.26.cloned.1.call-start = ((), (), s32[]{:S(2)}) async-start(), calls=%async_computation.26 | async-start | bytes 14155776 | tf_op jit(solution)/shard_map/reduce_scatter | solution.py:257
  382.5 68.1 %reduce-scatter.24.cloned.1.call-start = ((), (), s32[]{:S(2)}) async-start(), calls=%async_computation.25 | async-start | bytes 14155776 | tf_op jit(solution)/shard_map/reduce_scatter | solution.py:256
  394.3 58.0 %reduce-scatter.22.cloned.1.call-start = ((), (), s32[]{:S(2)}) async-start(), calls=%async_computation.24 | async-start | bytes 14155776 | tf_op jit(solution)/shard_map/reduce_scatter | solution.py:255
  406.1 65.3 %reduce-scatter.18.cloned.1.call-start = ((), (), s32[]{:S(2)}) async-start(), calls=%async_computation.22 | async-start | bytes 10616832 | tf_op jit(solution)/shard_map/reduce_scatter | solution.py:253
  450.5 538.7 %all-reduce.9.cloned.1.call-start = ((), (), s32[]{:S(2)}) async-start(), calls=%async_computation.27 | async-start | bytes 37748736 | tf_op jit(solution)/shard_map/psum | solution.py:263
  471.4 51.8 %copy-start.36 = (bf16[1,512,768]{2,1,0:T(8,128)(2,1)S(1)}, bf16[1,512,768]{2,1,0:T(8,128)(2,1)}, u32[]{:S(2)}) copy-start(bf16[1,512,768]{2,1,0:T(8,128)(2,1)} %get-tuple-element.110) | copy-start | bytes 2359300
  471.4 51.8 %copy-start.37 = (bf16[1,512,768]{2,1,0:T(8,128)(2,1)S(1)}, bf16[1,512,768]{2,1,0:T(8,128)(2,1)}, u32[]{:S(2)}) copy-start(bf16[1,512,768]{2,1,0:T(8,128)(2,1)} %get-tuple-element.111) | copy-start | bytes 2359300
  473.5 51.0 %copy-start.48 = (f32[512,768]{1,0:T(8,128)S(1)}, f32[512,768]{1,0:T(8,128)}, u32[]{:S(2)}) copy-start(f32[512,768]{1,0:T(8,128)} %get-tuple-element.122) | copy-start | bytes 4718596
  (107 other events, 746.5 us)
Sparse Core Ops, SparseCore 0:
  9.6 15.4 all-gather.13
  37.5 10.9 all-gather.17
  50.7 10.9 all-gather.15
  63.7 10.9 all-gather.29
  76.6 10.9 all-gather.27
  89.0 10.3 all-gather.19
  101.0 15.5 all-gather.21
  118.2 15.5 all-gather.23
  135.4 15.5 all-gather.25
  256.9 12.0 reduce-scatter.15
  278.0 12.0 reduce-scatter.11
  319.6 12.0 reduce-scatter.9
  363.1 12.0 reduce-scatter.13
  377.3 11.0 reduce-scatter.19
  390.6 18.9 reduce-scatter.25
  411.9 18.9 reduce-scatter.23
  433.1 19.0 reduce-scatter.21
  454.5 16.7 reduce-scatter.17
  477.8 511.3 all-reduce.8
where the time goes:
time: 1020 us; the launch traced here: 1010 us
  waiting for transfers between devices  493 us (48%)
  matrix products  300 us (29%)
  other arithmetic  91.5 us (9%)
  blocking collectives  56.6 us (6%)
  local copies, waits for them, and re-layouts  53.7 us (5%)
  between operations  16.6 us (2%)
    psum x1, waiting for transfers between devices, shards(): lax.psum((reduced[0], reduced[1], reduced[2], reduced[3], reduced[4], red...  455 us
    dot_general x10, matrix products, product_right_t(): lax.dot_general(left_side, right_side, (((1,), (1,)), ((), ())), preferre...  56.4 us
    dot_general x10, matrix products, product_left_t(): lax.dot_general(left_side, right_side, (((0,), (0,)), ((), ())), preferre...  48.4 us
    psum x1, blocking collectives, shards(): lax.psum((reduced[0], reduced[1], reduced[2], reduced[3], reduced[4], red...  45.6 us
    dot_general x10, matrix products, product(): return jnp.dot(left_side, right_side, preferred_element_type=jnp.float32)  44.1 us
    dot_general x2, matrix products, shards(): jnp.einsum('qhd,khd->hqk', context_heads, heads_of(value_rows), preferred...  39.3 us
    convert_element_type x2, other arithmetic, shards(): grad_scores = (score_scale * attn_probs * (grad_probs - jnp.sum(attn_prob...  34.6 us
    unnamed x238, local copies, waits for them, and re-layouts  32 us
  transfers between devices with their start and end apart: 19, of which 4 were waited for; matrix products, arithmetic and copies ran while one was open for 32% of the time, Pallas kernels for 0%

commit v1 on v0

v1 whole, which is shorter than its diff:
```python
import jax
import jax.numpy as jnp
from jax import lax
from jax.experimental import pallas as pl
from jax.experimental.pallas import tpu as pltpu
from jax.sharding import PartitionSpec as P

HEADS = 12
HEAD_DIM = 64


EPSILON = 1e-05


def doc_tables(doc_lengths, seq_len):
    doc_ends = jnp.cumsum(doc_lengths)
    doc_starts = doc_ends - doc_lengths
    places = jnp.arange(seq_len, dtype=jnp.int32)
    segment = jnp.sum((places[:, None] >= doc_ends[None, :]).astype(jnp.int32), axis=1)
    member = segment[:, None] == jnp.arange(doc_lengths.shape[0], dtype=jnp.int32)[None, :]
    begins = jnp.sum(jnp.where(member, doc_starts[None, :], 0), axis=1)
    return (segment, places - begins)


def rope_tables(positions):
    half_dim = HEAD_DIM // 2
    frequencies = 1000.0 ** (-2.0 * jnp.arange(half_dim, dtype=jnp.float32) / HEAD_DIM)
    angles = positions.astype(jnp.float32)[:, None] * frequencies[None, :]
    return (jnp.cos(angles), jnp.sin(angles))


def rotate(values, cosine_table, sine_table):
    row_count = values.shape[0]
    split_heads = values.reshape(row_count, HEADS, HEAD_DIM)
    first_half = split_heads[..., : HEAD_DIM // 2]
    second_half = split_heads[..., HEAD_DIM // 2 :]
    cosine_rows = cosine_table[:, None, :]
    sine_rows = sine_table[:, None, :]
    turned = jnp.concatenate(
        [
            first_half * cosine_rows - second_half * sine_rows,
            second_half * cosine_rows + first_half * sine_rows,
        ],
        axis=-1,
    )
    return turned.reshape(row_count, HEADS * HEAD_DIM)


def norm_forward(values, gain_vec, bias_vec):
    centre = values - jnp.mean(values, axis=-1, keepdims=True)
    inv_std = lax.rsqrt(jnp.mean(centre * centre, axis=-1, keepdims=True) + EPSILON)
    unit_rows = centre * inv_std
    return (unit_rows * gain_vec + bias_vec, unit_rows, inv_std)


def norm_back(grad_norm, unit_rows, inv_std):
    return inv_std * (
        grad_norm
        - jnp.mean(grad_norm, axis=-1, keepdims=True)
        - unit_rows * jnp.mean(grad_norm * unit_rows, axis=-1, keepdims=True)
    )


def heads_of(values):
    return values.reshape(values.shape[0], HEADS, HEAD_DIM)


def product(left_side, right_side):
    return jnp.dot(left_side, right_side, preferred_element_type=jnp.float32)


def product_left_t(left_side, right_side):
    return lax.dot_general(
        left_side, right_side, (((0,), (0,)), ((), ())), preferred_element_type=jnp.float32
    )


def product_right_t(left_side, right_side):
    return lax.dot_general(
        left_side, right_side, (((1,), (1,)), ((), ())), preferred_element_type=jnp.float32
    )


def masked_scores(query_heads, key_heads, same_doc, score_scale):
    raw_scores = jnp.einsum(
        "qhd,khd->hqk", query_heads, key_heads, preferred_element_type=jnp.float32
    )
    return jnp.where(same_doc[None], raw_scores * score_scale, -1e30)


CHUNKS = 16
PARTS = 3
PART_ROWS = 128
UNITS = 16
STEPS = 4
MESH = pl.DeviceIdType.MESH
BF16 = jnp.bfloat16
F32 = jnp.float32


def bit_of(value, weight):
    return lax.rem(lax.div(value, weight), 2)


def orders(chunk):
    rep = lax.axis_index("rep")
    odd = lax.rem(chunk, 2)
    first, second = 1 + odd, 2 - odd
    bits = {1: bit_of(rep, 1), 2: bit_of(rep, 2), 4: bit_of(rep, 4), 8: bit_of(rep, 8)}
    first_bit = bits[1] * (1 - odd) + bits[2] * odd
    second_bit = bits[2] * (1 - odd) + bits[1] * odd
    return (
        ((1, bits[1]), (2, bits[2]), (4, bits[4]), (8, bits[8])),
        ((2, bits[2]), (1, bits[1]), (4, bits[4]), (8, bits[8])),
        ((4, bits[4]), (first, first_bit), (second, second_bit), (8, bits[8])),
    )


def partner_of(weight, bit):
    return (lax.axis_index("rep") + weight * (1 - 2 * bit), lax.axis_index("fsdp"))


def other_core():
    return (lax.axis_index("rep"), 1 - lax.axis_index("fsdp"))


def region(ref, chunk, part, order, level, flip):
    rows = PART_ROWS >> min(level, STEPS - 1)
    start = part * PART_ROWS
    for step in range(level):
        bit = order[step][1]
        if flip and step == level - 1:
            bit = 1 - bit
        if step < STEPS - 1:
            start = start + bit * (PART_ROWS >> (step + 1))
        else:
            column = bit * (ref.shape[2] // 2)
    start = pl.multiple_of(start, 16)
    if level < STEPS:
        return (chunk, pl.ds(start, rows), slice(None))
    half = ref.shape[2] // 2
    return (chunk, pl.ds(start, rows), pl.ds(pl.multiple_of(column, 128), half))


def landing(ref, chunk, part, step):
    start = part * PART_ROWS + PART_ROWS - (PART_ROWS >> step)
    if step < STEPS - 1:
        return (chunk, pl.ds(start, PART_ROWS >> (step + 1)), slice(None))
    return (chunk, pl.ds(start, PART_ROWS >> step), pl.ds(0, ref.shape[2] // 2))


def halving_copy(refs, chunk, part, order, step):
    grads, halves, _, send_sems, recv_sems = refs
    return pltpu.make_async_remote_copy(
        src_ref=grads.at[region(grads, chunk, part, order, step + 1, True)],
        dst_ref=halves.at[landing(halves, chunk, part, step)],
        send_sem=send_sems.at[chunk, part, step],
        recv_sem=recv_sems.at[chunk, part, step],
        device_id=partner_of(*order[step]),
        device_id_type=MESH,
    )


def halving_add(refs, chunk, part, order, step):
    grads, halves = refs[:2]
    kept = region(grads, chunk, part, order, step + 1, False)
    theirs = halves[landing(halves, chunk, part, step)]
    grads[kept] = (grads[kept].astype(F32) + theirs.astype(F32)).astype(BF16)


def settle_copy(refs, chunk, part, order):
    grads, _, out, send_sems, _ = refs
    mine = region(grads, chunk, part, order, STEPS, False)
    return pltpu.make_async_copy(grads.at[mine], out.at[mine], send_sems.at[chunk, part, 2 * STEPS])


def doubling_copy(refs, chunk, part, order, step):
    _, _, out, send_sems, recv_sems = refs
    there = out.at[region(out, chunk, part, order, step + 1, False)]
    return pltpu.make_async_remote_copy(
        src_ref=there,
        dst_ref=there,
        send_sem=send_sems.at[chunk, part, STEPS + step],
        recv_sem=recv_sems.at[chunk, part, STEPS + step],
        device_id=partner_of(*order[step]),
        device_id_type=MESH,
    )


def rep_stage(refs, chunk, stage):
    for part, order in enumerate(orders(chunk)):
        if 1 <= stage <= STEPS:
            halving_copy(refs, chunk, part, order, stage - 1).wait()
            halving_add(refs, chunk, part, order, stage - 1)
        if stage > STEPS:
            doubling_copy(refs, chunk, part, order, 2 * STEPS - stage).wait()
        if stage < STEPS:
            halving_copy(refs, chunk, part, order, stage).start()
        elif stage < 2 * STEPS:
            if stage == STEPS:
                settle = settle_copy(refs, chunk, part, order)
                settle.start()
                settle.wait()
            doubling_copy(refs, chunk, part, order, 2 * STEPS - 1 - stage).start()


def greet():
    rep = lax.axis_index("rep")
    barrier = pltpu.get_barrier_semaphore()
    pl.semaphore_signal(barrier, inc=1, device_id=other_core(), device_id_type=MESH)
    for weight in (1, 2, 4, 8):
        there = partner_of(weight, bit_of(rep, weight))
        pl.semaphore_signal(barrier, inc=1, device_id=there, device_id_type=MESH)
    pl.semaphore_wait(barrier, 5)


def vector_copy(vectors, send_sems, recv_sems, step):
    rep = lax.axis_index("rep")
    if step == 0:
        there = other_core()
    else:
        weight = 1 << (step - 1)
        there = partner_of(weight, bit_of(rep, weight))
    return pltpu.make_async_remote_copy(
        src_ref=vectors.at[2 * step],
        dst_ref=vectors.at[2 * step + 1],
        send_sem=send_sems.at[step],
        recv_sem=recv_sems.at[step],
        device_id=there,
        device_id_type=MESH,
    )


VECTOR_STEPS = 5


def vector_stage(vectors, send_sems, recv_sems, stage):
    if stage > 0:
        vector_copy(vectors, send_sems, recv_sems, stage - 1).wait()
        vectors[2 * stage] = vectors[2 * stage - 2] + vectors[2 * stage - 1]
    if stage < VECTOR_STEPS:
        vector_copy(vectors, send_sems, recv_sems, stage).start()


def reduce_kernel(
    own, other, vec, out, vec_out, grads, halves, from_core, vectors,
    send_sems, recv_sems, core_send, core_recv, vec_send, vec_recv,
):
    refs = (grads, halves, out, send_sems, recv_sems)
    greet()
    vectors[0] = vec[...]

    def core_copy(chunk):
        return pltpu.make_async_remote_copy(
            src_ref=other.at[chunk],
            dst_ref=from_core.at[chunk],
            send_sem=core_send.at[chunk],
            recv_sem=core_recv.at[chunk],
            device_id=other_core(),
            device_id_type=MESH,
        )

    last = 2 * STEPS + 1

    def tick(t, carry):
        for stage in range(last, -1, -1):
            chunk = t - stage

            @pl.when((chunk >= 0) & (chunk < CHUNKS))
            def _():
                if stage == 0:
                    core_copy(chunk).start()
                if stage == 1:
                    core_copy(chunk).wait()
                    grads[chunk] = (own[chunk].astype(F32) + from_core[chunk].astype(F32)).astype(BF16)
                if stage >= 1:
                    rep_stage(refs, chunk, stage - 1)

        for stage in range(VECTOR_STEPS + 1):
            @pl.when(t == stage)
            def _():
                vector_stage(vectors, vec_send, vec_recv, stage)

        return carry

    lax.fori_loop(0, CHUNKS + last, tick, 0)
    vec_out[...] = vectors[2 * VECTOR_STEPS]


def all_reduce(own, other, vec):
    copies = pltpu.SemaphoreType.DMA
    return pl.pallas_call(
        reduce_kernel,
        out_shape=(jax.ShapeDtypeStruct(own.shape, BF16), jax.ShapeDtypeStruct(vec.shape, F32)),
        in_specs=[
            pl.BlockSpec(memory_space=pltpu.VMEM),
            pl.BlockSpec(memory_space=pl.ANY),
            pl.BlockSpec(memory_space=pltpu.VMEM),
        ],
        out_specs=(pl.BlockSpec(memory_space=pl.ANY), pl.BlockSpec(memory_space=pltpu.VMEM)),
        scratch_shapes=[
            pltpu.VMEM(own.shape, BF16),
            pltpu.VMEM(own.shape, BF16),
            pltpu.VMEM(own.shape, BF16),
            pltpu.VMEM((2 * VECTOR_STEPS + 1,) + vec.shape, F32),
            copies((CHUNKS, PARTS, 2 * STEPS + 1)),
            copies((CHUNKS, PARTS, 2 * STEPS)),
            copies((CHUNKS,)),
            copies((CHUNKS,)),
            copies((VECTOR_STEPS,)),
            copies((VECTOR_STEPS,)),
        ],
        compiler_params=pltpu.CompilerParams(collective_id=0, has_side_effects=True, vmem_limit_bytes=60 << 20),
    )(own, other, vec)


def to_sequence(block):
    return lax.all_to_all(block, "fsdp", split_axis=0, concat_axis=1, tiled=True)[0]


def to_positions(rows):
    return lax.all_to_all(rows[None], "fsdp", split_axis=1, concat_axis=0, tiled=True)


def row_halves(grad, core):
    rows, cols = grad.shape
    pieces = grad.reshape(2, rows // 768, 384, cols // 768, 768)
    pieces = jnp.moveaxis(pieces, 3, 1).reshape(2, -1, 384, 768).astype(BF16)
    return pieces


def shards(
    tokens,
    lengths,
    w_qkv,
    w_out,
    w_gate,
    w_up,
    w_down,
    norm1_gain,
    norm1_bias,
    norm2_gain,
    norm2_bias,
    cotangent,
):
    core = lax.axis_index("fsdp")
    stream = to_sequence(tokens)
    grad_out = to_sequence(cotangent).astype(F32)
    doc_lengths = lax.dynamic_index_in_dim(lengths, core, 0, keepdims=False)
    seq_len, model_width = stream.shape
    score_scale = HEAD_DIM ** (-0.5)

    def whole(block):
        return lax.all_gather(block, "fsdp", axis=0, tiled=True)

    w_qkv, w_out, w_gate, w_up, w_down = map(whole, (w_qkv, w_out, w_gate, w_up, w_down))
    vectors = whole(jnp.stack([norm1_gain, norm1_bias, norm2_gain, norm2_bias], axis=1)).astype(F32)
    gain_one, bias_one, gain_two, bias_two = (vectors[:, n] for n in range(4))
    stream_wide = stream.astype(F32)
    segment, positions = doc_tables(doc_lengths, seq_len)
    cosine_table, sine_table = rope_tables(positions)
    projected = product(stream, w_qkv)
    queries = rotate(projected[:, :model_width], cosine_table, sine_table).astype(BF16)
    key_rows = rotate(projected[:, model_width : 2 * model_width], cosine_table, sine_table).astype(BF16)
    value_rows = projected[:, 2 * model_width :].astype(BF16)
    same_doc = segment[:, None] == segment[None, :]
    scores = masked_scores(heads_of(queries), heads_of(key_rows), same_doc, score_scale)
    row_max = jnp.max(scores, axis=-1, keepdims=True)
    exp_scores = jnp.exp(scores - row_max)
    row_total = jnp.sum(exp_scores, axis=-1, keepdims=True)
    log_total = row_max + jnp.log(row_total)
    attn_low = (exp_scores / row_total).astype(BF16)
    context = jnp.einsum("hqk,khd->qhd", attn_low, heads_of(value_rows), preferred_element_type=F32)
    context = context.reshape(seq_len, model_width).astype(BF16)
    first_sum = stream_wide + product(context, w_out)
    normed, unit_one, inv_one = norm_forward(first_sum, gain_one, bias_one)
    normed_low = normed.astype(BF16)
    gate_act = product(normed_low, w_gate)
    up_act = product(normed_low, w_up)
    gate_sig = jax.nn.sigmoid(gate_act)
    gate_silu = gate_act * gate_sig
    hidden = (gate_silu * up_act).astype(BF16)
    second_sum = normed + product(hidden, w_down)
    result, unit_two, inv_two = norm_forward(second_sum, gain_two, bias_two)

    bias_two_grad = jnp.sum(grad_out, axis=0)
    gain_two_grad = jnp.sum(grad_out * unit_two, axis=0)
    grad_second = norm_back(grad_out * gain_two, unit_two, inv_two)
    grad_mixed = grad_second.astype(BF16)
    down_grad = product_left_t(hidden, grad_mixed)
    grad_hidden = product_right_t(grad_mixed, w_down)
    grad_gate_act = (grad_hidden * up_act * gate_sig * (1.0 + gate_act * (1.0 - gate_sig))).astype(BF16)
    grad_up_act = (grad_hidden * gate_silu).astype(BF16)
    gate_grad = product_left_t(normed_low, grad_gate_act)
    up_grad = product_left_t(normed_low, grad_up_act)
    grad_normed = grad_second + product_right_t(grad_gate_act, w_gate) + product_right_t(grad_up_act, w_up)
    bias_one_grad = jnp.sum(grad_normed, axis=0)
    gain_one_grad = jnp.sum(grad_normed * unit_one, axis=0)
    grad_first = norm_back(grad_normed * gain_one, unit_one, inv_one)
    grad_attended = grad_first.astype(BF16)
    out_grad = product_left_t(context, grad_attended)
    grad_context = product_right_t(grad_attended, w_out).astype(BF16)
    scores_again = masked_scores(heads_of(queries), heads_of(key_rows), same_doc, score_scale)
    attn_probs = jnp.exp(scores_again - log_total)
    context_heads = heads_of(grad_context)
    grad_probs = jnp.einsum("qhd,khd->hqk", context_heads, heads_of(value_rows), preferred_element_type=F32)
    grad_scores = (
        score_scale * attn_probs * (grad_probs - jnp.sum(attn_probs * grad_probs, axis=-1, keepdims=True))
    ).astype(BF16)
    grad_queries = jnp.einsum("hqk,khd->qhd", grad_scores, heads_of(key_rows), preferred_element_type=F32)
    grad_keys = jnp.einsum("hqk,qhd->khd", grad_scores, heads_of(queries), preferred_element_type=F32)
    grad_values = jnp.einsum("hqk,qhd->khd", attn_probs.astype(BF16), context_heads, preferred_element_type=F32)
    grad_projected = jnp.concatenate(
        [
            rotate(grad_queries.reshape(seq_len, model_width), cosine_table, -sine_table),
            rotate(grad_keys.reshape(seq_len, model_width), cosine_table, -sine_table),
            grad_values.reshape(seq_len, model_width),
        ],
        axis=1,
    ).astype(BF16)
    qkv_grad = product_left_t(stream, grad_projected)
    input_grad = grad_first + product_right_t(grad_projected, w_qkv)

    halves = [row_halves(grad, core) for grad in (down_grad, gate_grad, up_grad, out_grad, qkv_grad)]
    both = jnp.concatenate(halves, axis=1)
    own = lax.dynamic_index_in_dim(both, core, 0, keepdims=False)
    other = lax.dynamic_index_in_dim(both, 1 - core, 0, keepdims=False)
    zero = jnp.zeros_like(bias_one_grad)
    vec = jnp.stack([gain_one_grad, bias_one_grad, gain_two_grad, bias_two_grad, zero, zero, zero, zero])
    summed, vec_sum = all_reduce(own, other, vec)
    groups = lax.axis_size("rep") // UNITS
    if groups > 1:
        alike = [[UNITS * g + n for g in range(groups)] for n in range(UNITS)]
        summed = lax.psum(summed, "rep", axis_index_groups=alike)
        vec_sum = lax.psum(vec_sum, "rep", axis_index_groups=alike)
    summed = summed.astype(F32)

    def wide(first, count):
        return jnp.moveaxis(summed[first : first + count], 0, 1).reshape(384, -1)

    vec_own = lax.dynamic_slice_in_dim(vec_sum, core * 384, 384, axis=1)
    return (
        to_positions(result.astype(BF16)),
        to_positions(input_grad),
        wide(13, 3),
        wide(12, 1),
        wide(4, 4),
        wide(8, 4),
        summed[:4].reshape(-1, model_width),
        vec_own[0],
        vec_own[1],
        vec_own[2],
        vec_own[3],
    )


def solution(mesh):
    placed = (
        P("rep", "fsdp", None),
        P("rep", None),
        P("fsdp", None),
        P("fsdp", None),
        P("fsdp", None),
        P("fsdp", None),
        P("fsdp", None),
        P("fsdp"),
        P("fsdp"),
        P("fsdp"),
        P("fsdp"),
        P("rep", "fsdp", None),
    )
    return jax.shard_map(
        shards,
        mesh=mesh,
        in_specs=placed,
        out_specs=(
            P("rep", "fsdp", None),
            P("rep", "fsdp", None),
            P("fsdp", None),
            P("fsdp", None),
            P("fsdp", None),
            P("fsdp", None),
            P("fsdp", None),
            P("fsdp"),
            P("fsdp"),
            P("fsdp"),
            P("fsdp"),
        ),
        check_vma=False,
    )
```

time: 1020 us -> 746 us (0.73)
  waiting for transfers between devices: 493 us -> 4.43 us
  Pallas kernels: 0 us -> 165 us
  local copies, waits for them, and re-layouts: 53.7 us -> 172 us
  matrix products: 300 us -> 251 us
  blocking collectives: 56.6 us -> 10.1 us
  starting transfers between devices: 1.35 us -> 14 us
  other arithmetic: 91.5 us -> 104 us
    psum x1 -> x0, waiting for transfers between devices: 455 us -> none  [shards(): lax.psum((reduced[0], reduced[1], reduced[2], reduced[3], reduced[4], red...]
    pallas_call x0 -> x1, Pallas kernels: none -> 165 us  [all_reduce(): pl.pallas_call(reduce_kernel, out_shape=(jax.ShapeDtypeStruct(own.shape,...]
    psum x1 -> x0, blocking collectives: 45.6 us -> none  [shards(): lax.psum((reduced[0], reduced[1], reduced[2], reduced[3], reduced[4], red...]
    convert_element_type x6 -> x5, local copies, waits for them, and re-layouts: 4.93 us -> 36.7 us  [the longest x4 34.6 us: row_halves(): pieces = jnp.moveaxis(pieces, 3, 1).reshape(2, -1, 384, 768).astype(BF16)]
    transpose x0 -> x5, local copies, waits for them, and re-layouts: none -> 25.5 us  [wide(): return jnp.moveaxis(summed[first:first + count], 0, 1).reshape(384, -1)]
    reduce_scatter x9 -> x0, waiting for transfers between devices: 20.8 us -> none  [the longest x1 19 us: shards(): lax.psum_scatter(totals[0], 'fsdp', scatter_dimension=0, tiled=True)]
    unnamed x238 -> x112, local copies, waits for them, and re-layouts: 32 us -> 51.2 us
    broadcast_in_dim x0 -> x2, local copies, waits for them, and re-layouts: none -> 17.1 us  [to_positions(): rows[None]]
  transfers between devices with their start and end apart: 19 -> 8, of which waited for: 4 -> 1; matrix products, arithmetic and copies ran while one was open for 32% -> 22% of each run, Pallas kernels for 0% -> 0%
where the time goes in v1:
time: 746 us; the launch traced here: 734 us
  matrix products  251 us (34%)
  local copies, waits for them, and re-layouts  172 us (23%)
  Pallas kernels  165 us (22%)
  other arithmetic  104 us (14%)
  between operations  15 us (2%)
  starting transfers between devices  14 us (2%)
  blocking collectives  10.1 us (1%)
    pallas_call x1, Pallas kernels, all_reduce(): pl.pallas_call(reduce_kernel, out_shape=(jax.ShapeDtypeStruct(own.shape,...  165 us
    unnamed x112, local copies, waits for them, and re-layouts  51.2 us
    dot_general x5, matrix products, product_right_t(): lax.dot_general(left_side, right_side, (((1,), (1,)), ((), ())), preferre...  45 us
    dot_general x5, matrix products, product(): return jnp.dot(left_side, right_side, preferred_element_type=jnp.float32)  44.3 us
    convert_element_type x1, other arithmetic, shards(): grad_scores = (score_scale * attn_probs * (grad_probs - jnp.sum(attn_prob...  40.8 us
    dot_general x1, matrix products, shards(): jnp.einsum('qhd,khd->hqk', context_heads, heads_of(value_rows), preferred...  35.2 us
    convert_element_type x4, local copies, waits for them, and re-layouts, row_halves(): pieces = jnp.moveaxis(pieces, 3, 1).reshape(2, -1, 384, 768).astype(BF16)  34.6 us
    dot_general x5, matrix products, product_left_t(): lax.dot_general(left_side, right_side, (((0,), (0,)), ((), ())), preferre...  34.3 us
  transfers between devices with their start and end apart: 8, of which 1 were waited for; matrix products, arithmetic and copies ran while one was open for 22% of the time, Pallas kernels for 0%

profile of v1, /device:TPU:0, one launch (start us, length us, event | category | flops | bytes accessed | tf_op | source)
XLA Modules:
  0.0 734.5 jit_solution(9259939805779303262)
XLA Ops:
  55.2 21.1 %fusion.6 = (f32[12,1024]{1,0:T(8,128)S(1)}, f32[12,1024,1024]{1,2,0:T(8,128)}) fusion(pred[1024,1024]{0,1:T(8,128)(4,1)S(1)} %broadcast_compare_fusion, bf16[1024,12,32]{0,2,1:T(8,128)(2,1)S(1)} %get-tuple-element.106, bf16[1024,12,32]{0,2,1:T(8,128)(2,1)S(1)} %get-tuple-element.107, bf16[1024,12,32]{0,2,1:T(8,128)(2,1)S(1)} %get-tuple-element.99, ...), kind=kOutput, calls=%fused_computation.11 | convolution fusion | flops 1654640640 | bytes 54575104 | tf_op jit(solution)/shard_map/qhd,khd->hqk/dot_general | solution.py:85
  76.3 22.4 %fusion = f32[12,1024]{1,0:T(8,128)S(1)} fusion(f32[12,1024]{1,0:T(8,128)S(1)} %get-tuple-element.111, f32[12,1024,1024]{1,2,0:T(8,128)} %get-tuple-element.112, pred[1024,1024]{0,1:T(8,128)(4,1)S(1)} %broadcast_compare_fusion), kind=kLoop, calls=%fused_computation.6 | loop fusion | flops 50319360 | bytes 51478528 | tf_op jit(solution)/shard_map/reduce_sum | solution.py:370
  99.4 21.6 %fusion.15 = bf16[12,64,1024]{2,1,0:T(8,128)(2,1)} fusion(bf16[1024,12,64]{0,2,1:T(8,128)(2,1)S(1)} %bitcast.131, f32[12,1024]{1,0:T(8,128)S(1)} %fusion, f32[12,1024]{1,0:T(8,128)S(1)} %get-tuple-element.111, f32[12,1024,1024]{1,2,0:T(8,128)} %get-tuple-element.112, pred[1024,1024]{0,1:T(8,128)(4,1)S(1)} %broadcast_compare_fusion), kind=kOutput, calls=%fused_computation.57 | convolution fusion | flops 1674313728 | bytes 54624256 | tf_op jit(solution)/shard_map/hqk,khd->qhd/dot_general | solution.py:373
  126.8 10.1 %fusion.50 = f32[1024,3072]{1,0:T(8,128)} fusion(bf16[1024,768]{0,1:T(8,128)(2,1)} %fusion.10, bf16[768,3072]{1,0:T(8,128)(2,1)} %all-gather.10.cloned.1.call-done), kind=kOutput, calls=%fused_computation.129 | convolution fusion | flops 4831838208 | bytes 18874368 | tf_op jit(solution)/shard_map/dot_general | solution.py:69
  136.9 14.5 %multiply_convert_fusion.3 = (bf16[1024,3072]{1,0:T(8,128)(2,1)}, f32[1024,3072]{1,0:T(8,128)}) fusion(f32[1024,3072]{1,0:T(8,128)} %fusion.50, bf16[1024,768]{0,1:T(8,128)(2,1)} %fusion.10, bf16[768,3072]{1,0:T(8,128)(2,1)} %all-gather.12.cloned.1.call-done), kind=kOutput, calls=%fused_computation.14 | convolution fusion | flops 4850712576 | bytes 37748736 | tf_op jit(solution)/shard_map/dot_general | solution.py:69
  151.4 9.3 %fusion.48 = (f32[1024]{0:T(1024)S(1)}, f32[1024,768]{0,1:T(8,128)S(1)}) fusion(bf16[1024,3072]{1,0:T(8,128)(2,1)} %get-tuple-element.115, bf16[3072,768]{1,0:T(8,128)(2,1)} %all-gather.14.cloned.1.call-done, f32[768]{0:T(1024)S(1)} %get-tuple-element.84, f32[768]{0:T(1024)S(1)} %get-tuple-element.85, f32[1024]{0:T(1024)S(1)} %add_rsqrt_fusion.1, ...), kind=kOutput, calls=%fused_computation.127 | convolution fusion | flops 4836555776 | bytes 17319936 | tf_op jit(solution)/shard_map/dot_general | solution.py:69
  173.6 20.2 %multiply_convert_fusion.1 = (bf16[1024,3072]{1,0:T(8,128)(2,1)}, bf16[1024,3072]{1,0:T(8,128)(2,1)}) fusion(f32[1024,3072]{1,0:T(8,128)} %fusion.50, f32[1024,3072]{1,0:T(8,128)} %get-tuple-element.116, bf16[3072,768]{1,0:T(8,128)(2,1)} %all-gather.14.cloned.1.call-done, f32[1024,768]{0,1:T(8,128)} %copy-done.11), kind=kOutput, calls=%fused_computation.12 | convolution fusion | flops 4873519104 | bytes 45613056 | tf_op jit(solution)/shard_map/dot_general | solution.py:79
  193.8 9.1 %convolution_convert_fusion = bf16[768,3072]{1,0:T(8,128)(2,1)} fusion(bf16[1024,768]{0,1:T(8,128)(2,1)} %fusion.10, bf16[1024,3072]{1,0:T(8,128)(2,1)} %get-tuple-element.86), kind=kOutput, calls=%fused_computation.19 | convolution fusion | flops 4834197504 | bytes 12582912 | tf_op jit(solution)/shard_map/dot_general | solution.py:73
  229.0 21.3 %fusion.12 = bf16[12,64,1024]{2,1,0:T(8,128)(2,1)} fusion(bf16[1024,12,64]{0,2,1:T(8,128)(2,1)S(1)} %bitcast.143, f32[12,1024]{1,0:T(8,128)S(1)} %copy-done.23, f32[12,1024,1024]{1,2,0:T(8,128)} %get-tuple-element.112, pred[1024,1024]{0,1:T(8,128)(4,1)S(1)} %copy-done.2), kind=kOutput, calls=%fused_computation.55 | convolution fusion | flops 1661730816 | bytes 54575104 | tf_op jit(solution)/shard_map/hqk,qhd->khd/dot_general | solution.py:412
  250.4 35.2 %multiply_reduce_fusion = (f32[12,1024]{1,0:T(8,128)S(1)}, f32[12,1024,1024]{1,2,0:T(8,128)}) fusion(f32[12,1024]{1,0:T(8,128)S(1)} %copy-done.23, f32[12,1024,1024]{1,2,0:T(8,128)} %get-tuple-element.112, pred[1024,1024]{0,1:T(8,128)(4,1)S(1)} %copy-done.2, bf16[1024,12,64]{0,2,1:T(8,128)(2,1)} %bitcast.144, bf16[1024,12,64]{0,2,1:T(8,128)(2,1)S(1)} %bitcast.132), kind=kOutput, calls=%fused_computation.1 | convolution fusion | flops 1673515008 | bytes 104955904 | tf_op jit(solution)/shard_map/qhd,khd->hqk/dot_general | solution.py:406
  285.6 40.8 %multiply_convert_fusion = bf16[12,1024,1024]{1,2,0:T(8,128)(2,1)} fusion(f32[12,1024,1024]{1,2,0:T(8,128)} %get-tuple-element.121, f32[12,1024]{1,0:T(8,128)S(1)} %get-tuple-element.120, f32[12,1024]{1,0:T(8,128)S(1)} %copy-done.23, f32[12,1024,1024]{1,2,0:T(8,128)} %get-tuple-element.112, pred[1024,1024]{0,1:T(8,128)(4,1)S(1)} %copy-done.2), kind=kLoop, calls=%fused_computation | loop fusion | flops 88080384 | bytes 126976000 | tf_op jit(solution)/shard_map/convert_element_type | solution.py:409
  326.4 13.1 %convolution_bitcast_fusion = f32[1024,12,64]{0,2,1:T(8,128)S(1)} fusion(bf16[12,1024,1024]{1,2,0:T(8,128)(2,1)} %multiply_convert_fusion, bf16[1024,12,32]{0,2,1:T(8,128)(2,1)} %copy-done.16, bf16[1024,12,32]{0,2,1:T(8,128)(2,1)} %copy-done.15), kind=kOutput, calls=%fused_computation.53 | convolution fusion | flops 1613758464 | bytes 29884416 | tf_op jit(solution)/shard_map/hqk,qhd->khd/dot_general | solution.py:411
  339.5 14.8 %convolution_bitcast_fusion.1 = f32[1024,12,64]{0,2,1:T(8,128)} fusion(bf16[12,1024,1024]{1,2,0:T(8,128)(2,1)} %multiply_convert_fusion, bf16[1024,12,32]{0,2,1:T(8,128)(2,1)} %copy-done.13, bf16[1024,12,32]{0,2,1:T(8,128)(2,1)} %copy-done.14), kind=kOutput, calls=%fused_computation.54 | convolution fusion | flops 1613758464 | bytes 29884416 | tf_op jit(solution)/shard_map/hqk,khd->qhd/dot_general | solution.py:410
  354.3 9.7 %convert_element_type.153 = bf16[2,1,384,4,768]{4,3,2,0,1:T(4,128)(2,1)} reshape(bf16[768,3072]{1,0:T(8,128)(2,1)} %convolution_convert_fusion.1) | data formatting | bytes 9437184 | tf_op jit(solution)/shard_map/convert_element_type | solution.py:328
  364.1 9.7 %convert_element_type.157 = bf16[2,1,384,4,768]{4,3,2,0,1:T(4,128)(2,1)} reshape(bf16[768,3072]{1,0:T(8,128)(2,1)} %convolution_convert_fusion) | data formatting | bytes 9437184 | tf_op jit(solution)/shard_map/convert_element_type | solution.py:328
  382.0 8.7 %fusion.8 = bf16[768,2304]{0,1:T(8,128)(2,1)S(1)} fusion(bf16[1024,768]{1,0:T(8,128)(2,1)} %bitcast, bf16[1024,768]{0,1:T(8,128)(2,1)S(1)} %bitcast.152, bf16[1024,768]{0,1:T(8,128)(2,1)S(1)} %bitcast.140, bf16[1024,768]{0,1:T(8,128)(2,1)S(1)} %bitcast.138), kind=kOutput, calls=%fused_computation.28 | convolution fusion | flops 3639803904 | bytes 9830400 | tf_op jit(solution)/shard_map/dot_general | solution.py:73
  393.8 12.1 %copy.137 = bf16[2,1,384,3,768]{4,2,3,0,1:T(8,128)(2,1)} copy(bf16[2,1,384,3,768]{2,0,4,3,1:T(2,128)(2,1)} %convert_element_type.164) | data formatting | bytes 7077888 | tf_op jit(solution)/shard_map/convert_element_type | solution.py:328
  419.8 14.1 %dynamic-slice_bitcast_fusion = (bf16[16,384,768]{2,1,0:T(8,128)(2,1)}, bf16[16,384,768]{2,1,0:T(8,128)(2,1)}) fusion(bf16[2,16,384,768]{3,2,1,0:T(8,128)(2,1)} %bitcast_dynamic-update-slice_fusion.2, s32[]{:T(128)S(6)} %select_n.24, s32[]{:T(128)S(6)} %select_n.21), kind=kLoop, calls=%fused_computation.17 | loop fusion | bytes 37748744 | tf_op jit(solution)/shard_map/jit(dynamic_index_in_dim)/squeeze | solution.py:427
  434.6 164.6 %shard_map.203 = (bf16[16,384,768]{2,1,0:T(8,128)(2,1)}, f32[8,768]{1,0:T(8,128)}) custom-call(bf16[16,384,768]{2,1,0:T(8,128)(2,1)} %get-tuple-element.91.own, bf16[16,384,768]{2,1,0:T(8,128)(2,1)} %get-tuple-element.90.other, f32[8,768]{1,0:T(8,128)} %stack.43.vec), custom_call_target="tpu_custom_call" | custom-call | tf_op jit(solution)/shard_map/pallas_call | solution.py:292
  603.5 12.2 %convert_element_type.167 = f32[16,384,768]{2,1,0:T(8,128)} convert(bf16[16,384,768]{2,1,0:T(8,128)(2,1)} %get-tuple-element.13) | non-fusion elementwise | flops 4718592 | bytes 28311552 | tf_op jit(solution)/shard_map/convert_element_type | solution.py:436
  628.4 8.5 %copy.125 = bf16[1,1024,768]{2,0,1:T(2,128)(2,1)} copy(bf16[1,1024,768]{1,2,0:T(8,128)(2,1)} %get-tuple-element.103) | data formatting | bytes 3145728 | tf_op jit(solution)/shard_map/broadcast_in_dim | solution.py:322
  637.5 12.4 %reduce.23 = bf16[1024,768]{1,0:T(8,128)(2,1)} reduce(bf16[1024,1,768]{2,1,0:T(2,128)(2,1)} %bitcast.127, bf16[]{:T(256)} %broadcast.205), dimensions={1}, to_apply=%bitcast.89.reduce_sub_computation | reduce | bytes 3145730
  667.5 8.5 %add_bitcast_fusion = f32[1,1024,768]{1,2,0:T(8,128)} fusion(f32[1024,768]{0,1:T(8,128)S(1)} %copy-done.10, bf16[768,2304]{1,0:T(8,128)(2,1)} %all-gather.6.cloned.1.call-done, bf16[1024,768]{0,1:T(8,128)(2,1)} %bitcast.151, bf16[1024,768]{0,1:T(8,128)(2,1)} %bitcast.141, bf16[1024,768]{0,1:T(8,128)(2,1)S(1)} %bitcast.139), kind=kOutput, calls=%fused_computation.34 | convolution fusion | flops 3638820864 | bytes 14548992 | tf_op jit(solution)/shard_map/dot_general | solution.py:79
  676.0 8.5 %copy.133 = f32[1,1024,768]{2,0,1:T(1,128)} copy(f32[1,1024,768]{1,2,0:T(8,128)} %add_bitcast_fusion) | data formatting | bytes 6291456 | tf_op jit(solution)/shard_map/broadcast_in_dim | solution.py:322
  (206 shorter events, 196.6 us)
Async XLA Ops:
  7.2 25.0 %all-gather.6.cloned.1.call-start = ((), (), s32[]{:S(2)}) async-start(), calls=%async_computation.4 | async-start | bytes 5308416 | tf_op jit(solution)/shard_map/all_gather | solution.py:354
  7.9 113.0 %all-gather.8.cloned.1.call-start = ((), (), s32[]{:S(2)}) async-start(), calls=%async_computation.5 | async-start | bytes 1769472 | tf_op jit(solution)/shard_map/all_gather | solution.py:354
  8.7 118.1 %all-gather.10.cloned.1.call-start = ((), (), s32[]{:S(2)}) async-start(), calls=%async_computation.6 | async-start | bytes 7077888 | tf_op jit(solution)/shard_map/all_gather | solution.py:354
  9.4 127.5 %all-gather.12.cloned.1.call-start = ((), (), s32[]{:S(2)}) async-start(), calls=%async_computation.7 | async-start | bytes 7077888 | tf_op jit(solution)/shard_map/all_gather | solution.py:354
  10.0 8.3 %all-to-all-start.2 = ((bf16[2,512,768]{2,1,0:T(8,128)(2,1)}), bf16[2,512,768]{2,1,0:T(8,128)(2,1)S(1)}, u32[]{:S(2)}, u32[]{:S(2)}) async-start(bf16[2,512,768]{2,1,0:T(8,128)(2,1)} %param.23), calls=%async_computation.2 | async-start | bytes 3145728 | tf_op jit(solution)/shard_map/all_to_all | solution.py:318
  13.8 137.5 %all-gather.14.cloned.1.call-start = ((), (), s32[]{:S(2)}) async-start(), calls=%async_computation.8 | async-start | bytes 7077888 | tf_op jit(solution)/shard_map/all_gather | solution.py:354
  17.5 81.9 %copy-start.1 = (pred[1024,1024]{0,1:T(8,128)(4,1)}, pred[1024,1024]{0,1:T(8,128)(4,1)S(1)}, u32[]{:S(2)}) copy-start(pred[1024,1024]{0,1:T(8,128)(4,1)S(1)} %broadcast_compare_fusion) | copy-start | bytes 3145732
  18.3 10.5 %copy-start.25 = (f32[768]{0:T(1024)}, f32[768]{0:T(1024)S(1)}, u32[]{:S(2)}) copy-start(f32[768]{0:T(1024)S(1)} %get-tuple-element.82) | copy-start | bytes 9220
  18.4 8.0 %all-to-all-start = ((bf16[2,512,768]{2,1,0:T(8,128)(2,1)}), bf16[2,512,768]{2,1,0:T(8,128)(2,1)}, u32[]{:S(2)}, u32[]{:S(2)}) async-start(bf16[2,512,768]{2,1,0:T(8,128)(2,1)} %param.12), calls=%async_computation | async-start | bytes 3145728 | tf_op jit(solution)/shard_map/all_to_all | solution.py:318
  32.2 19.1 %copy-start.21 = (f32[1024,32]{0,1:T(8,128)}, f32[1024,32]{0,1:T(8,128)S(1)}, u32[]{:S(2)}) copy-start(f32[1024,32]{0,1:T(8,128)S(1)} %get-tuple-element.110) | copy-start | bytes 393220
  55.2 21.1 %copy-start.13 = (bf16[1024,12,32]{0,2,1:T(8,128)(2,1)}, bf16[1024,12,32]{0,2,1:T(8,128)(2,1)S(1)}, u32[]{:S(2)}) copy-start(bf16[1024,12,32]{0,2,1:T(8,128)(2,1)S(1)} %get-tuple-element.106) | copy-start | bytes 2359300
  55.2 21.1 %copy-start.14 = (bf16[1024,12,32]{0,2,1:T(8,128)(2,1)}, bf16[1024,12,32]{0,2,1:T(8,128)(2,1)S(1)}, u32[]{:S(2)}) copy-start(bf16[1024,12,32]{0,2,1:T(8,128)(2,1)S(1)} %get-tuple-element.107) | copy-start | bytes 2359300
  55.2 21.1 %copy-start.15 = (bf16[1024,12,32]{0,2,1:T(8,128)(2,1)}, bf16[1024,12,32]{0,2,1:T(8,128)(2,1)S(1)}, u32[]{:S(2)}) copy-start(bf16[1024,12,32]{0,2,1:T(8,128)(2,1)S(1)} %get-tuple-element.98) | copy-start | bytes 2359300
  55.2 21.1 %copy-start.16 = (bf16[1024,12,32]{0,2,1:T(8,128)(2,1)}, bf16[1024,12,32]{0,2,1:T(8,128)(2,1)S(1)}, u32[]{:S(2)}) copy-start(bf16[1024,12,32]{0,2,1:T(8,128)(2,1)S(1)} %get-tuple-element.99) | copy-start | bytes 2359300
  76.3 23.0 %copy-start.6 = (bf16[1024,768]{0,1:T(8,128)(2,1)S(1)}, bf16[1024,768]{0,1:T(8,128)(2,1)}, u32[]{:S(2)}) copy-start(bf16[1024,768]{0,1:T(8,128)(2,1)} %copy.121) | copy-start | bytes 4718596
  193.8 9.2 %copy-start.39 = (bf16[1024,3072]{1,0:T(8,128)(2,1)S(1)}, bf16[1024,3072]{1,0:T(8,128)(2,1)}, u32[]{:S(2)}) copy-start(bf16[1024,3072]{1,0:T(8,128)(2,1)} %get-tuple-element.87) | copy-start | bytes 18874372
  193.8 16.1 %slice-start.2 = ((s8[4718592]{0:T(1024)(128)(4,1)}), s8[4194304]{0:T(1024)(128)(4,1)S(1)}, s32[]{:S(2)}) async-start(s8[4718592]{0:T(1024)(128)(4,1)} %bitcast.135), calls=%async_computation.11 | async-start | bytes 8388608
  203.0 13.9 %slice-start.4 = ((s8[4718592]{0:T(1024)(128)(4,1)}), s8[4194304]{0:T(1024)(128)(4,1)S(1)}, s32[]{:S(2)}) async-start(s8[4718592]{0:T(1024)(128)(4,1)} %bitcast.147), calls=%async_computation.13 | async-start | bytes 8388608
  203.0 13.9 %slice-start.6 = ((s8[6291456]{0:T(1024)(128)(4,1)}), s8[4194304]{0:T(1024)(128)(4,1)S(1)}, s32[]{:S(2)}) async-start(s8[6291456]{0:T(1024)(128)(4,1)} %bitcast.153), calls=%async_computation.15 | async-start | bytes 8388608
  229.0 21.3 %copy-start.7 = (bf16[1024,768]{0,1:T(8,128)(2,1)S(1)}, bf16[1024,768]{0,1:T(8,128)(2,1)}, u32[]{:S(2)}) copy-start(bf16[1024,768]{0,1:T(8,128)(2,1)} %copy.121) | copy-start | bytes 4718596
  339.5 14.8 %copy-start.29 = (f32[768]{0:T(1024)S(1)}, f32[768]{0:T(1024)}, u32[]{:S(2)}) copy-start(f32[768]{0:T(1024)} %get-tuple-element.70) | copy-start | bytes 9220
  393.8 17.4 %slice-start = ((s8[4718592]{0:T(1024)(128)(4,1)}), s8[524288]{0:T(1024)(128)(4,1)S(1)}, s32[]{:S(2)}) async-start(s8[4718592]{0:T(1024)(128)(4,1)} %bitcast.121), calls=%async_computation.9 | async-start | bytes 1048576
  419.8 14.2 %copy-start.30 = (f32[1,768]{1,0:T(1,128)S(1)}, f32[1,768]{1,0:T(1,128)}, u32[]{:S(2)}) copy-start(f32[1,768]{1,0:T(1,128)} %stack.41) | copy-start | bytes 9220
  684.5 39.2 %all-to-all-start.3 = ((f32[1,1024,768]{2,0,1:T(1,128)}), f32[1,1024,768]{2,0,1:T(1,128)}, u32[]{:S(2)}, u32[]{:S(2)}) async-start(f32[1,1024,768]{2,0,1:T(1,128)} %copy.133), calls=%async_computation.3 | async-start | bytes 6291456 | tf_op jit(solution)/shard_map/all_to_all | solution.py:322
  (34 other events, 131.6 us)
Sparse Core Ops, SparseCore 0:
  9.6 16.0 all-gather.5
  27.2 9.6 all-gather.7
  38.5 15.5 all-gather.9
  55.6 15.6 all-gather.11
  72.6 15.6 all-gather.13

commit v2 on v1

v2 whole, which is shorter than its diff:
```python
import jax
import jax.numpy as jnp
from jax import lax
from jax.experimental import pallas as pl
from jax.experimental.pallas import tpu as pltpu
from jax.sharding import PartitionSpec as P

HEADS = 12
HEAD_DIM = 64


EPSILON = 1e-05


def doc_tables(doc_lengths, seq_len):
    doc_ends = jnp.cumsum(doc_lengths)
    doc_starts = doc_ends - doc_lengths
    places = jnp.arange(seq_len, dtype=jnp.int32)
    segment = jnp.sum((places[:, None] >= doc_ends[None, :]).astype(jnp.int32), axis=1)
    member = segment[:, None] == jnp.arange(doc_lengths.shape[0], dtype=jnp.int32)[None, :]
    begins = jnp.sum(jnp.where(member, doc_starts[None, :], 0), axis=1)
    return (segment, places - begins)


def rope_tables(positions):
    half_dim = HEAD_DIM // 2
    frequencies = 1000.0 ** (-2.0 * jnp.arange(half_dim, dtype=jnp.float32) / HEAD_DIM)
    angles = positions.astype(jnp.float32)[:, None] * frequencies[None, :]
    return (jnp.cos(angles), jnp.sin(angles))


CHUNKS = 16
PARTS = 3
PART_ROWS = 128
UNITS = 16
STEPS = 4
MESH = pl.DeviceIdType.MESH
BF16 = jnp.bfloat16
F32 = jnp.float32


def bit_of(value, weight):
    return lax.rem(lax.div(value, weight), 2)


def orders(chunk):
    rep = lax.axis_index("rep")
    odd = lax.rem(chunk, 2)
    first, second = 1 + odd, 2 - odd
    bits = {1: bit_of(rep, 1), 2: bit_of(rep, 2), 4: bit_of(rep, 4), 8: bit_of(rep, 8)}
    first_bit = bits[1] * (1 - odd) + bits[2] * odd
    second_bit = bits[2] * (1 - odd) + bits[1] * odd
    return (
        ((1, bits[1]), (2, bits[2]), (4, bits[4]), (8, bits[8])),
        ((2, bits[2]), (1, bits[1]), (4, bits[4]), (8, bits[8])),
        ((4, bits[4]), (first, first_bit), (second, second_bit), (8, bits[8])),
    )


def partner_of(weight, bit):
    return (lax.axis_index("rep") + weight * (1 - 2 * bit), lax.axis_index("fsdp"))


def other_core():
    return (lax.axis_index("rep"), 1 - lax.axis_index("fsdp"))


def region(ref, chunk, part, order, level, flip):
    rows = PART_ROWS >> min(level, STEPS - 1)
    start = part * PART_ROWS
    for step in range(level):
        bit = order[step][1]
        if flip and step == level - 1:
            bit = 1 - bit
        if step < STEPS - 1:
            start = start + bit * (PART_ROWS >> (step + 1))
        else:
            column = bit * (ref.shape[2] // 2)
    start = pl.multiple_of(start, 16)
    if level < STEPS:
        return (chunk, pl.ds(start, rows), slice(None))
    half = ref.shape[2] // 2
    return (chunk, pl.ds(start, rows), pl.ds(pl.multiple_of(column, 128), half))


def landing(ref, chunk, part, step):
    start = part * PART_ROWS + PART_ROWS - (PART_ROWS >> step)
    chunk = lax.rem(chunk, ref.shape[0])
    if step < STEPS - 1:
        return (chunk, pl.ds(start, PART_ROWS >> (step + 1)), slice(None))
    return (chunk, pl.ds(start, PART_ROWS >> step), pl.ds(0, ref.shape[2] // 2))


def halving_copy(refs, chunk, part, order, step):
    grads, halves, _, send_sems, recv_sems = refs
    return pltpu.make_async_remote_copy(
        src_ref=grads.at[region(grads, chunk, part, order, step + 1, True)],
        dst_ref=halves.at[landing(halves, chunk, part, step)],
        send_sem=send_sems.at[chunk, part, step],
        recv_sem=recv_sems.at[chunk, part, step],
        device_id=partner_of(*order[step]),
        device_id_type=MESH,
    )


def halving_add(refs, chunk, part, order, step):
    grads, halves = refs[:2]
    kept = region(grads, chunk, part, order, step + 1, False)
    theirs = halves[landing(halves, chunk, part, step)]
    grads[kept] = (grads[kept].astype(F32) + theirs.astype(F32)).astype(BF16)


def settle_copy(refs, chunk, part, order):
    grads, _, out, send_sems, _ = refs
    mine = region(grads, chunk, part, order, STEPS, False)
    return pltpu.make_async_copy(grads.at[mine], out.at[mine], send_sems.at[chunk, part, 2 * STEPS])


def doubling_copy(refs, chunk, part, order, step):
    _, _, out, send_sems, recv_sems = refs
    there = out.at[region(out, chunk, part, order, step + 1, False)]
    return pltpu.make_async_remote_copy(
        src_ref=there,
        dst_ref=there,
        send_sem=send_sems.at[chunk, part, STEPS + step],
        recv_sem=recv_sems.at[chunk, part, STEPS + step],
        device_id=partner_of(*order[step]),
        device_id_type=MESH,
    )


def rep_stage(refs, chunk, stage):
    for part, order in enumerate(orders(chunk)):
        if 1 <= stage <= STEPS:
            halving_copy(refs, chunk, part, order, stage - 1).wait()
            halving_add(refs, chunk, part, order, stage - 1)
        if stage > STEPS:
            doubling_copy(refs, chunk, part, order, 2 * STEPS - stage).wait()
        if stage < STEPS:
            halving_copy(refs, chunk, part, order, stage).start()
        elif stage < 2 * STEPS:
            if stage == STEPS:
                settle = settle_copy(refs, chunk, part, order)
                settle.start()
                settle.wait()
            doubling_copy(refs, chunk, part, order, 2 * STEPS - 1 - stage).start()


def greet():
    rep = lax.axis_index("rep")
    barrier = pltpu.get_barrier_semaphore()
    pl.semaphore_signal(barrier, inc=1, device_id=other_core(), device_id_type=MESH)
    for weight in (1, 2, 4, 8):
        there = partner_of(weight, bit_of(rep, weight))
        pl.semaphore_signal(barrier, inc=1, device_id=there, device_id_type=MESH)
    pl.semaphore_wait(barrier, 5)


def vector_copy(vectors, send_sems, recv_sems, step):
    rep = lax.axis_index("rep")
    if step == 0:
        there = other_core()
    else:
        weight = 1 << (step - 1)
        there = partner_of(weight, bit_of(rep, weight))
    return pltpu.make_async_remote_copy(
        src_ref=vectors.at[2 * step],
        dst_ref=vectors.at[2 * step + 1],
        send_sem=send_sems.at[step],
        recv_sem=recv_sems.at[step],
        device_id=there,
        device_id_type=MESH,
    )


VECTOR_STEPS = 5


def vector_stage(vectors, send_sems, recv_sems, stage):
    if stage > 0:
        vector_copy(vectors, send_sems, recv_sems, stage - 1).wait()
        vectors[2 * stage] = vectors[2 * stage - 2] + vectors[2 * stage - 1]
    if stage < VECTOR_STEPS:
        vector_copy(vectors, send_sems, recv_sems, stage).start()


SEQ_ROWS = 512
NEG = -1e30
FEATURES = 128
SPLIT_LANE = 8


def nn(left, right):
    return jnp.dot(left, right, preferred_element_type=F32)


def nt(left, right):
    return lax.dot_general(left, right, (((1,), (1,)), ((), ())), preferred_element_type=F32)


def tn(left, right):
    return lax.dot_general(left, right, (((0,), (0,)), ((), ())), preferred_element_type=F32)


def aligned(start, size, multiple=None):
    return pl.ds(pl.multiple_of(start, multiple or size), size)


def lanes():
    return lax.broadcasted_iota(jnp.int32, (1, 128), 1)


def head_mask(values, first):
    low = lanes() < HEAD_DIM
    zero = jnp.zeros_like(values)
    return jnp.where(low, values, zero) if first else jnp.where(low, zero, values)


def turn(values, cosines, sines):
    first = lax.rem(lanes(), HEAD_DIM) < HEAD_DIM // 2
    swapped = jnp.where(first, pltpu.roll(values, 96, 1), pltpu.roll(values, 32, 1))
    return values * cosines + swapped * sines


def split_lanes(base, values):
    high = values.astype(BF16).astype(F32)
    middle = (values - high).astype(BF16).astype(F32)
    low = values - high - middle
    lane = lanes()
    out = jnp.where(lane == SPLIT_LANE, high, base)
    out = jnp.where(lane == SPLIT_LANE + 1, middle, out)
    return jnp.where(lane == SPLIT_LANE + 2, low, out).astype(BF16)


def row_mean(values):
    return jnp.mean(values, axis=1, keepdims=True)


def forward_kernel(
    tokens, cotangent, w_qkv, w_out, w_gate, w_up, w_down, norms, query_marks, key_marks, cosines, sines,
    q_out, k_out, v_out, context_out, features_out, low_out, unit_out, inv_out, slope_gate_out, slope_up_out,
    hidden_out, grad_second_out, mixed_out, activations_out, vec_out,
    norms_out, wq_out, wo_out, wg_out, wu_out, wd_out,
    x, g, wq, wo, wg, wu, wd, nv, qs, ks, vs, ctx, total, low, key_aug, value_aug, pieces, acts, seconds,
    send_sems, recv_sems, own_sems, save_sems, act_sems,
):
    rep = lax.axis_index("rep")
    core = lax.axis_index("fsdp")
    there = (rep, 1 - core)
    seq, width = x.shape
    half = seq // 2

    barrier = pltpu.get_barrier_semaphore()
    pl.semaphore_signal(barrier, inc=1, device_id=there, device_id_type=MESH)
    pl.semaphore_wait(barrier, 1)

    def rows_of(ref, block):
        return ref.at[aligned(core * block, block)]

    exchanges = (
        (tokens.at[core], tokens.at[1 - core], rows_of(x, half)),
        (w_qkv, w_qkv, rows_of(wq, w_qkv.shape[0])),
        (w_out, w_out, rows_of(wo, w_out.shape[0])),
        (norms, norms, nv.at[core]),
        (w_gate, w_gate, rows_of(wg, w_gate.shape[0])),
        (w_up, w_up, rows_of(wu, w_up.shape[0])),
        (w_down, w_down, rows_of(wd, w_down.shape[0])),
        (cotangent.at[core], cotangent.at[1 - core], rows_of(g, half)),
    )

    def copies(number):
        mine, theirs, place = exchanges[number]
        return (
            pltpu.make_async_copy(mine, place, own_sems.at[number]),
            pltpu.make_async_remote_copy(
                src_ref=theirs,
                dst_ref=place,
                send_sem=send_sems.at[number],
                recv_sem=recv_sems.at[number],
                device_id=there,
                device_id_type=MESH,
            ),
        )

    for number in range(len(exchanges)):
        for copy in copies(number):
            copy.start()

    def arrived(number):
        for copy in copies(number):
            copy.wait()

    def save(source, target, number):
        copy = pltpu.make_async_copy(source, target, save_sems.at[number])
        copy.start()
        return copy

    arrived(0)
    arrived(1)
    tile = 512
    for n, out in enumerate((qs, ks, vs)):
        for r in range(seq // tile):
            rows = pl.ds(r * tile, tile)
            product_rows = nn(x[rows, :], wq[:, pl.ds(n * width, width)])
            if n == 2:
                out[rows, :] = product_rows.astype(BF16)
                continue
            for pair in range(width // 128):
                cols = slice(pair * 128, pair * 128 + 128)
                turned = turn(product_rows[:, cols], cosines[rows, :], sines[rows, :]).astype(BF16)
                if n == 0:
                    turned = turned * jnp.asarray(HEAD_DIM ** (-0.5), BF16)
                out[rows, cols] = turned
    saves = {0: save(qs, q_out, 0), 1: save(ks, k_out, 1), 2: save(vs, v_out, 2)}

    saves[7] = save(wq, wq_out, 7)

    block = 256
    steps = [(a, r) for r in range(seq // block) for a in range(2)]

    def pair_step(pair, carry):
        cols = aligned(pair * 128, 128)
        key_aug[:, :128] = ks[:, cols]
        key_aug[:, 128:] = key_marks[...]
        for a in range(2):
            value_aug[a, :, :128] = head_mask(vs[:, cols], a == 0)
            value_aug[a, :, 128:] = jnp.ones((seq, 128), BF16)

        def scores_of(a, r):
            rows = pl.ds(r * block, block)
            query = jnp.concatenate([head_mask(qs[rows, cols], a == 0), query_marks[rows, :]], axis=1)
            return nt(query, key_aug[...])

        scores = scores_of(*steps[0])
        parts = [None, None]
        for number, (a, r) in enumerate(steps):
            rows = pl.ds(r * block, block)
            upcoming = scores_of(*steps[number + 1]) if number + 1 < len(steps) else None
            row_max = jnp.max(scores, axis=1, keepdims=True)
            probs = jnp.exp(scores - row_max).astype(BF16)
            summed = nn(probs, value_aug[a])
            row_total = summed[:, 128:]
            parts[a] = summed[:, :128] / row_total
            lse = row_max + jnp.log(row_total)
            features_out[2 * pair + a, rows, :] = split_lanes(query_marks[rows, :].astype(F32), -lse)
            if a == 1:
                ctx[rows, cols] = (parts[0] + parts[1]).astype(BF16)
            scores = upcoming
        return carry

    lax.fori_loop(0, HEADS // 2, pair_step, 0)
    saves[3] = save(ctx, context_out, 3)

    arrived(2)
    arrived(3)

    def vector(n):
        return jnp.concatenate([nv[0, n : n + 1, :], nv[1, n : n + 1, :]], axis=1)

    for r in range(seq // block):
        rows = pl.ds(r * block, block)
        first_sum = x[rows, :].astype(F32) + nn(ctx[rows, :], wo[...])
        centre = first_sum - row_mean(first_sum)
        inv = lax.rsqrt(row_mean(centre * centre) + EPSILON)
        unit = centre * inv
        normed = unit * vector(0) + vector(1)
        seconds[rows, :] = unit
        inv_out[rows, :] = jnp.broadcast_to(inv, (block, 128))
        total[rows, :] = normed
        low[rows, :] = normed.astype(BF16)
    saves[4] = save(seconds, unit_out, 4)
    saves[5] = save(low, low_out, 5)
    saves[8] = save(wo, wo_out, 8)

    arrived(4)
    arrived(5)
    arrived(6)
    for number, (source, target) in enumerate(((wg, wg_out), (wu, wu_out), (wd, wd_out))):
        saves[9 + number] = save(source, target, 9 + number)
    columns = pieces.shape[3]
    row_tiles = seq // tile
    count = row_tiles * (wg.shape[1] // columns)
    outs = (slope_gate_out, slope_up_out, hidden_out)

    def piece_copy(number, n):
        slot = lax.rem(number, 2)
        rows = aligned(lax.rem(number, row_tiles) * tile, tile)
        cols = aligned(lax.div(number, row_tiles) * columns, columns)
        return pltpu.make_async_copy(pieces.at[slot, n], outs[n].at[rows, cols], act_sems.at[slot, n])

    def feed_step(number, carry):
        slot = lax.rem(number, 2)
        rows = aligned(lax.rem(number, row_tiles) * tile, tile)
        cols = aligned(lax.div(number, row_tiles) * columns, columns)

        @pl.when(number >= 2)
        def _():
            for n in range(3):
                piece_copy(number - 2, n).wait()

        gate = nn(low[rows, :], wg[:, cols])
        up = nn(low[rows, :], wu[:, cols])
        gate_sig = 0.5 + 0.5 * jnp.tanh(0.5 * gate)
        gate_silu = gate * gate_sig
        pieces[slot, 0] = (up * gate_sig * (1.0 + gate * (1.0 - gate_sig))).astype(BF16)
        pieces[slot, 1] = gate_silu.astype(BF16)
        hidden = (gate_silu * up).astype(BF16)
        pieces[slot, 2] = hidden
        for n in range(3):
            piece_copy(number, n).start()
        total[rows, :] += nn(hidden, wd[cols, :])
        return carry

    lax.fori_loop(0, count, feed_step, 0)

    arrived(7)
    saves[2].wait()
    saves[4].wait()
    gain_two, bias_two = vector(2), vector(3)
    bias_sum = jnp.zeros((1, width), F32)
    gain_sum = jnp.zeros((1, width), F32)
    for r in range(seq // block):
        rows = pl.ds(r * block, block)
        second_sum = total[rows, :]
        centre = second_sum - row_mean(second_sum)
        inv = lax.rsqrt(row_mean(centre * centre) + EPSILON)
        unit = centre * inv
        acts[rows, :] = (unit * gain_two + bias_two).astype(BF16)
        grad_out = g[rows, :].astype(F32)
        bias_sum += jnp.sum(grad_out, axis=0, keepdims=True)
        gain_sum += jnp.sum(grad_out * unit, axis=0, keepdims=True)
        scaled = grad_out * gain_two
        grad_second = inv * (scaled - row_mean(scaled) - unit * row_mean(scaled * unit))
        seconds[rows, :] = grad_second
        vs[rows, :] = grad_second.astype(BF16)
    norms_out[...] = nv[...]
    vec_out[...] = jnp.zeros_like(vec_out)
    vec_out[2:3, :] = gain_sum
    vec_out[3:4, :] = bias_sum
    saves[4] = save(seconds, grad_second_out, 4)
    saves[2] = save(vs, mixed_out, 2)

    mine = pltpu.make_async_copy(rows_of(acts, half), activations_out.at[core], save_sems.at[6])
    mine.start()
    theirs = pltpu.make_async_remote_copy(
        src_ref=acts.at[aligned((1 - core) * half, half)],
        dst_ref=activations_out.at[core],
        send_sem=send_sems.at[len(exchanges)],
        recv_sem=recv_sems.at[len(exchanges)],
        device_id=there,
        device_id_type=MESH,
    )
    theirs.start()
    for copy in saves.values():
        copy.wait()
    for number in range(2):
        for n in range(3):
            piece_copy(count - 2 + number, n).wait()
    mine.wait()
    theirs.wait()


def forward(tokens, cotangent, weights, norms, query_marks, key_marks, cosines, sines):
    w_qkv, w_out, w_gate, w_up, w_down = weights
    seq, width = 2 * tokens.shape[1], tokens.shape[2]
    hidden_width = w_gate.shape[1]
    dma = pltpu.SemaphoreType.DMA
    vmem = pl.BlockSpec(memory_space=pltpu.VMEM)
    hbm = pl.BlockSpec(memory_space=pl.ANY)

    def shape(*dims, dtype=BF16):
        return jax.ShapeDtypeStruct(dims, dtype)

    def full(shard):
        return pltpu.VMEM((2 * shard.shape[0], shard.shape[1]), BF16)

    rows = shape(seq, width)
    wide = shape(seq, hidden_width)
    return pl.pallas_call(
        forward_kernel,
        out_shape=(
            rows, rows, rows, rows, shape(HEADS, seq, FEATURES), rows, shape(seq, width, dtype=F32),
            shape(seq, 128, dtype=F32), wide, wide, wide, shape(seq, width, dtype=F32), rows,
            shape(*tokens.shape), shape(8, width, dtype=F32), shape(2, *norms.shape, dtype=F32),
        )
        + tuple(shape(2 * shard.shape[0], shard.shape[1]) for shard in weights),
        in_specs=[hbm] * 8 + [vmem] * 4,
        out_specs=(hbm, hbm, hbm, hbm, vmem, hbm, hbm, vmem, hbm, hbm, hbm, hbm, hbm, hbm, vmem, vmem) + (hbm,) * 5,
        scratch_shapes=[
            pltpu.VMEM((seq, width), BF16),
            pltpu.VMEM((seq, width), BF16),
            full(w_qkv), full(w_out), full(w_gate), full(w_up), full(w_down),
            pltpu.VMEM((2,) + norms.shape, F32),
            pltpu.VMEM((seq, width), BF16),
            pltpu.VMEM((seq, width), BF16),
            pltpu.VMEM((seq, width), BF16),
            pltpu.VMEM((seq, width), BF16),
            pltpu.VMEM((seq, width), F32),
            pltpu.VMEM((seq, width), BF16),
            pltpu.VMEM((seq, 256), BF16),
            pltpu.VMEM((2, seq, 256), BF16),
            pltpu.VMEM((2, 3, 512, 768), BF16),
            pltpu.VMEM((seq, width), BF16),
            pltpu.VMEM((seq, width), F32),
            dma((9,)), dma((9,)), dma((8,)), dma((12,)), dma((2, 3)),
        ],
        compiler_params=pltpu.CompilerParams(collective_id=1, has_side_effects=True, vmem_limit_bytes=62 << 20),
    )(tokens, cotangent, w_qkv, w_out, w_gate, w_up, w_down, norms, query_marks, key_marks, cosines, sines)


RING = 4
HALVES_RING = 8


def backward_kernel(
    tokens, context, low, mixed, hidden, slope_gate, slope_up, grad_second, unit, inv, norms, q_in, k_in, v_in,
    features, key_marks, cosines, sines, vec, wq, wo, wg, wu, wd,
    out, input_grad_out, vec_out,
    grads, halves, from_core, to_core, vectors, arena, total, key_aug, value_aug, delta_aug, dkey, dvalue, wide,
    send_sems, recv_sems, core_send, core_recv, vec_send, vec_recv, load_sems, input_sems,
):
    rep = lax.axis_index("rep")
    core = lax.axis_index("fsdp")
    seq, width = total.shape
    shard = width // 2
    refs = (grads, halves, out, send_sems, recv_sems)
    greet()

    def load(slot, source, target=None):
        return pltpu.make_async_copy(source, arena.at[slot] if target is None else target, load_sems.at[slot])

    def square(slot):
        return arena.at[slot, pl.ds(0, width), :]

    def sided(slot, source, first, second):
        return (
            pltpu.make_async_copy(
                source.at[:, aligned(first, shard, 128)], arena.at[slot, :, pl.ds(0, shard)], load_sems.at[slot]
            ),
            pltpu.make_async_copy(
                source.at[:, aligned(second, shard, 128)], arena.at[slot, :, pl.ds(shard, shard)], input_sems.at[slot]
            ),
        )

    def begin(loads):
        for one in loads if isinstance(loads, tuple) else (loads,):
            one.start()

    def finish(loads):
        for one in loads if isinstance(loads, tuple) else (loads,):
            one.wait()

    def core_copy(chunk):
        slot = lax.rem(chunk, RING)
        return pltpu.make_async_remote_copy(
            src_ref=to_core.at[slot],
            dst_ref=from_core.at[slot],
            send_sem=core_send.at[slot],
            recv_sem=core_recv.at[slot],
            device_id=other_core(),
            device_id_type=MESH,
        )

    def emit(chunk, left, right):
        slot = lax.rem(chunk, RING)

        @pl.when(chunk >= RING)
        def _():
            core_copy(chunk - RING).wait_send()

        to_core[slot] = tn(arena[left, :, shard:], arena[right]).astype(BF16)
        core_copy(chunk).start()
        grads[chunk] = tn(arena[left, :, :shard], arena[right]).astype(BF16)

    def absorb(chunk):
        core_copy(chunk).wait_recv()
        slot = lax.rem(chunk, RING)
        grads[chunk] = (grads[chunk].astype(F32) + from_core[slot].astype(F32)).astype(BF16)

    def slot_work(k):
        for stage in range(2 * STEPS, -1, -1):
            entered = k - stage

            @pl.when((entered >= 0) & (entered <= CHUNKS) & (entered != CHUNKS - 3))
            def _():
                rep_stage(refs, entered - lax.div(entered, CHUNKS - 3), stage)

    MIXED, LOW, SLOPE_GATE, SLOPE_UP, HIDDEN, GATE, UP, WD, WG, WU = range(10)
    blocks = wg.shape[1] // width

    def block_loads(j):
        cols = aligned(j * width, width)
        return {
            SLOPE_GATE: load(SLOPE_GATE, slope_gate.at[:, cols]),
            SLOPE_UP: load(SLOPE_UP, slope_up.at[:, cols]),
            WD: load(WD, wd.at[cols, :], square(WD)),
            WG: load(WG, wg.at[:, cols], square(WG)),
            WU: load(WU, wu.at[:, cols], square(WU)),
            HIDDEN: sided(
                HIDDEN,
                hidden,
                core * (wd.shape[0] // 2) + j * shard,
                (1 - core) * (wd.shape[0] // 2) + j * shard,
            ),
        }

    first_loads = block_loads(0)
    mixed_load = load(MIXED, mixed)
    low_load = sided(LOW, low, core * shard, (1 - core) * shard)
    second_load = load(10, grad_second, total)
    for one in (mixed_load, first_loads[WD], first_loads[SLOPE_GATE], first_loads[SLOPE_UP], first_loads[HIDDEN],
                low_load, first_loads[WG], first_loads[WU], second_load):
        begin(one)
    vectors[0] = vec[...]
    finish(mixed_load)

    tile = 512

    def feed_step(j, carry):
        loads = block_loads(j)
        upcoming = block_loads(j + 1)

        def renew(*slots):
            @pl.when(j + 1 < blocks)
            def _():
                for slot in slots:
                    begin(upcoming[slot])

        for slot in (WD, SLOPE_GATE, SLOPE_UP):
            finish(loads[slot])
        for r in range(seq // tile):
            rows = pl.ds(r * tile, tile)
            grad_hidden = nt(arena[MIXED, rows, :], arena[WD, :width, :])
            arena[GATE, rows, :] = (grad_hidden * arena[SLOPE_GATE, rows, :].astype(F32)).astype(BF16)
            arena[UP, rows, :] = (grad_hidden * arena[SLOPE_UP, rows, :].astype(F32)).astype(BF16)
        renew(WD, SLOPE_GATE, SLOPE_UP)
        finish(loads[HIDDEN])
        emit(3 * j, HIDDEN, MIXED)
        renew(HIDDEN)

        @pl.when(j > 0)
        def _():
            absorb(3 * j - 1)
            slot_work(2 * j - 1)

        @pl.when(j == 0)
        def _():
            finish(low_load)
            finish(second_load)

        emit(3 * j + 1, LOW, GATE)
        finish(loads[WG])
        for r in range(seq // tile):
            rows = pl.ds(r * tile, tile)
            total[rows, :] += nt(arena[GATE, rows, :], arena[WG, :width, :])
        renew(WG)
        absorb(3 * j)
        slot_work(2 * j)
        emit(3 * j + 2, LOW, UP)
        finish(loads[WU])
        for r in range(seq // tile):
            rows = pl.ds(r * tile, tile)
            total[rows, :] += nt(arena[UP, rows, :], arena[WU, :width, :])
        renew(WU)
        absorb(3 * j + 1)
        return carry

    lax.fori_loop(0, blocks, feed_step, 0)

    CONTEXT, SIDED_CONTEXT, WO, ATTENDED, GRAD_CONTEXT, Q, K, V, DQ, DK, DV, TOKENS, WQ = range(13)
    chunk = 3 * blocks
    loads = {
        CONTEXT: load(CONTEXT, context),
        SIDED_CONTEXT: sided(SIDED_CONTEXT, context, core * shard, (1 - core) * shard),
        WO: load(WO, wo, square(WO)),
        Q: load(Q, q_in),
        K: load(K, k_in),
        V: load(V, v_in),
        TOKENS: sided(TOKENS, tokens, core * shard, (1 - core) * shard),
        WQ: load(WQ, wq.at[:, pl.ds(0, width)], square(WQ)),
    }
    for slot in (SIDED_CONTEXT, WO, CONTEXT, Q, K, V, TOKENS, WQ):
        begin(loads[slot])
    absorb(chunk - 1)
    gain_one = jnp.concatenate([norms[0, 0:1, :], norms[1, 0:1, :]], axis=1)
    bias_sum = jnp.zeros((1, width), F32)
    gain_sum = jnp.zeros((1, width), F32)
    block = 256
    for r in range(seq // block):
        rows = pl.ds(r * block, block)
        grad_normed = total[rows, :]
        unit_rows = unit[rows, :]
        bias_sum += jnp.sum(grad_normed, axis=0, keepdims=True)
        gain_sum += jnp.sum(grad_normed * unit_rows, axis=0, keepdims=True)
        scaled = grad_normed * gain_one
        grad_first = inv[rows, 0:1] * (scaled - row_mean(scaled) - unit_rows * row_mean(scaled * unit_rows))
        total[rows, :] = grad_first
        arena[ATTENDED, rows, :] = grad_first.astype(BF16)
    vectors[0, 0:1, :] = gain_sum
    vectors[0, 1:2, :] = bias_sum
    finish(loads[SIDED_CONTEXT])
    emit(chunk, SIDED_CONTEXT, ATTENDED)
    finish(loads[WO])
    for r in range(seq // tile):
        rows = pl.ds(r * tile, tile)
        arena[GRAD_CONTEXT, rows, :] = nt(arena[ATTENDED, rows, :], arena[WO, :width, :]).astype(BF16)
    absorb(chunk)
    first_slot = 2 * blocks - 1
    slot_work(first_slot)
    for slot in (CONTEXT, Q, K, V):
        finish(loads[slot])

    steps = [(a, r) for r in range(seq // block) for a in range(2)]
    ones = jnp.where((lanes() >= SPLIT_LANE) & (lanes() < SPLIT_LANE + 3), 1.0, 0.0)

    def pair_step(pair, carry):
        cols = aligned(pair * 128, 128)
        key_aug[:, :128] = arena[K, :, cols]
        key_aug[:, 128:] = (key_marks[...].astype(F32) + ones).astype(BF16)
        value_aug[:, :128] = arena[V, :, cols]
        value_aug[:, 128:] = jnp.broadcast_to(ones, (seq, 128)).astype(BF16)
        delta = arena[GRAD_CONTEXT, :, cols].astype(F32) * arena[CONTEXT, :, cols].astype(F32)
        for a in range(2):
            row_delta = jnp.sum(head_mask(delta, a == 0), axis=1, keepdims=True)
            delta_aug[a, :, :128] = head_mask(arena[GRAD_CONTEXT, :, cols], a == 0)
            delta_aug[a, :, 128:] = split_lanes(jnp.zeros((seq, 128), F32), -row_delta)

        def products_of(a, r):
            rows = pl.ds(r * block, block)
            query = jnp.concatenate([head_mask(arena[Q, rows, cols], a == 0), features[2 * pair + a, rows, :]], axis=1)
            return nt(query, key_aug[...]), nt(delta_aug[a, rows, :], value_aug[...])

        upcoming = products_of(*steps[0])
        for number, (a, r) in enumerate(steps):
            rows = pl.ds(r * block, block)
            scores, grad_probs = upcoming
            upcoming = products_of(*steps[number + 1]) if number + 1 < len(steps) else None
            probs = jnp.exp(scores)
            grad_scores = (probs * grad_probs).astype(BF16)
            probs = probs.astype(BF16)
            dquery = nn(grad_scores, head_mask(key_aug[:, :128], a == 0))
            dkey_term = tn(grad_scores, head_mask(arena[Q, rows, cols], a == 0))
            dvalue_term = tn(probs, delta_aug[a, rows, :128])
            if number == 0:
                dkey[...] = dkey_term
                dvalue[...] = dvalue_term
            else:
                dkey[...] += dkey_term
                dvalue[...] += dvalue_term
            if a == 0:
                wide[...] = dquery
            else:
                dquery = (wide[...] + dquery) * (HEAD_DIM ** (-0.5))
                arena[DQ, rows, cols] = turn(dquery, cosines[rows, :], -sines[rows, :]).astype(BF16)
        arena[DK, :, cols] = turn(dkey[...], cosines[...], -sines[...]).astype(BF16)
        arena[DV, :, cols] = dvalue[...].astype(BF16)
        slot_work(first_slot + 1 + pair)
        for stage in range(VECTOR_STEPS + 1):

            @pl.when(pair == stage)
            def _():
                vector_stage(vectors, vec_send, vec_recv, stage)

        return carry

    lax.fori_loop(0, HEADS // 2, pair_step, 0)
    k = first_slot + 1 + HEADS // 2

    finish(loads[TOKENS])
    following = load(WQ, wq.at[:, pl.ds(0, width)], square(WQ))
    for n, slot in enumerate((DQ, DK, DV)):
        emit(chunk + 1 + n, TOKENS, slot)
        finish(following)
        for r in range(seq // tile):
            rows = pl.ds(r * tile, tile)
            total[rows, :] += nt(arena[slot, rows, :], arena[WQ, :width, :])
        if n < 2:
            following = load(WQ, wq.at[:, pl.ds((n + 1) * width, width)], square(WQ))
            following.start()
        absorb(chunk + 1 + n)
        slot_work(k + n)

    half = seq // 2
    mine = pltpu.make_async_copy(total.at[aligned(core * half, half)], input_grad_out.at[core], load_sems.at[13])
    theirs = pltpu.make_async_remote_copy(
        src_ref=total.at[aligned((1 - core) * half, half)],
        dst_ref=input_grad_out.at[core],
        send_sem=core_send.at[RING],
        recv_sem=core_recv.at[RING],
        device_id=other_core(),
        device_id_type=MESH,
    )
    mine.start()
    theirs.start()
    vec_out[...] = vectors[2 * VECTOR_STEPS]

    def drain(k, carry):
        slot_work(k)
        return carry

    lax.fori_loop(k + 3, CHUNKS + 2 * STEPS + 1, drain, 0)
    mine.wait()
    theirs.wait()
    for number in range(RING):
        core_copy(CHUNKS - RING + number).wait_send()


def backward(tokens, saved, norms, key_marks, cosines, sines, vec, weights, outs):
    context, low, mixed, hidden, slope_gate, slope_up, grad_second, unit, inv, q, k, v, features = saved
    seq, width = tokens.shape
    dma = pltpu.SemaphoreType.DMA
    vmem = pl.BlockSpec(memory_space=pltpu.VMEM)
    hbm = pl.BlockSpec(memory_space=pl.ANY)
    chunks = (CHUNKS, width // 2, width)
    return pl.pallas_call(
        backward_kernel,
        out_shape=(
            jax.ShapeDtypeStruct(chunks, BF16),
            jax.ShapeDtypeStruct(outs, F32),
            jax.ShapeDtypeStruct(vec.shape, F32),
        ),
        in_specs=[hbm] * 8 + [vmem] * 3 + [hbm] * 3 + [vmem] * 5 + [hbm] * 5,
        out_specs=(hbm, hbm, vmem),
        scratch_shapes=[
            pltpu.VMEM(chunks, BF16),
            pltpu.VMEM((HALVES_RING,) + chunks[1:], BF16),
            pltpu.VMEM((RING,) + chunks[1:], BF16),
            pltpu.VMEM((RING,) + chunks[1:], BF16),
            pltpu.VMEM((2 * VECTOR_STEPS + 1,) + vec.shape, F32),
            pltpu.VMEM((13, seq, width), BF16),
            pltpu.VMEM((seq, width), F32),
            pltpu.VMEM((seq, 256), BF16),
            pltpu.VMEM((seq, 256), BF16),
            pltpu.VMEM((2, seq, 256), BF16),
            pltpu.VMEM((seq, 128), F32),
            pltpu.VMEM((seq, 128), F32),
            pltpu.VMEM((256, 128), F32),
            dma((CHUNKS, PARTS, 2 * STEPS + 1)),
            dma((CHUNKS, PARTS, 2 * STEPS)),
            dma((RING + 1,)),
            dma((RING + 1,)),
            dma((VECTOR_STEPS,)),
            dma((VECTOR_STEPS,)),
            dma((14,)),
            dma((14,)),
        ],
        compiler_params=pltpu.CompilerParams(collective_id=0, has_side_effects=True, vmem_limit_bytes=62 << 20),
    )(tokens, context, low, mixed, hidden, slope_gate, slope_up, grad_second, unit, inv, norms, q, k, v,
      features, key_marks, cosines, sines, vec, *weights)


def widen_kernel(summed, qkv, out, gate, up, down):
    step = pl.program_id(0)
    values = summed[0].astype(F32)
    turn_of = lax.rem(step, 3)
    fed = step < CHUNKS - 4
    for ref, now in (
        (down, fed & (turn_of == 0)),
        (gate, fed & (turn_of == 1)),
        (up, fed & (turn_of == 2)),
        (out, step == CHUNKS - 4),
        (qkv, step > CHUNKS - 4),
    ):

        @pl.when(now)
        def _():
            ref[...] = values


def widen(summed):
    rows, cols = summed.shape[1:]
    fed = CHUNKS - 4

    def shape(high, across):
        return jax.ShapeDtypeStruct((rows * high, cols * across), F32)

    def spec(place):
        return pl.BlockSpec((rows, cols), place)

    def turn_of(step):
        return lax.div(jnp.minimum(step, fed - 1), 3)

    return pl.pallas_call(
        widen_kernel,
        grid=(CHUNKS,),
        out_shape=(shape(1, 3), shape(1, 1), shape(1, 4), shape(1, 4), shape(4, 1)),
        in_specs=[pl.BlockSpec((1, rows, cols), lambda step: (step, 0, 0))],
        out_specs=(
            spec(lambda step: (0, jnp.maximum(step - fed - 1, 0))),
            spec(lambda step: (0, 0)),
            spec(lambda step: (0, turn_of(step))),
            spec(lambda step: (0, turn_of(step))),
            spec(lambda step: (turn_of(step), 0)),
        ),
    )(summed)


def shards(
    tokens,
    lengths,
    w_qkv,
    w_out,
    w_gate,
    w_up,
    w_down,
    norm1_gain,
    norm1_bias,
    norm2_gain,
    norm2_bias,
    cotangent,
):
    core = lax.axis_index("fsdp")
    shard = norm1_gain.shape[0]
    seq_len = 2 * tokens.shape[1]
    doc_lengths = lax.dynamic_index_in_dim(lengths, core, 0, keepdims=False)
    segment, positions = doc_tables(doc_lengths, seq_len)
    cosine_table, sine_table = rope_tables(positions)
    cosines = jnp.concatenate([cosine_table] * 4, axis=1)
    sines = jnp.concatenate([-sine_table, sine_table] * 2, axis=1)
    columns = jnp.arange(FEATURES, dtype=jnp.int32)[None, :]
    same = segment[:, None] == columns
    query_marks = same.astype(BF16)
    key_marks = jnp.where(same | (columns >= SPLIT_LANE), 0.0, NEG).astype(BF16)
    zero = jnp.zeros_like(norm1_gain)
    norms = jnp.stack([norm1_gain, norm1_bias, norm2_gain, norm2_bias, zero, zero, zero, zero]).astype(F32)

    weights = (w_qkv, w_out, w_gate, w_up, w_down)
    (q, k, v, context, features, low, unit, inv, slope_gate, slope_up, hidden, grad_second, mixed, activations,
     vec, norms, *weights) = forward(tokens, cotangent, weights, norms, query_marks, key_marks, cosines, sines)
    stream = lax.all_to_all(tokens, "fsdp", split_axis=0, concat_axis=1, tiled=True)[0]
    saved = (context, low, mixed, hidden, slope_gate, slope_up, grad_second, unit, inv, q, k, v, features)
    summed, input_grad, vec_sum = backward(
        stream, saved, norms, key_marks, cosines, sines, vec, weights, tokens.shape
    )
    groups = lax.axis_size("rep") // UNITS
    if groups > 1:
        alike = [[UNITS * g + n for g in range(groups)] for n in range(UNITS)]
        summed = lax.psum(summed, "rep", axis_index_groups=alike)
        vec_sum = lax.psum(vec_sum, "rep", axis_index_groups=alike)
    vec_own = lax.dynamic_slice_in_dim(vec_sum, core * shard, shard, axis=1)
    return (activations, input_grad, *widen(summed), vec_own[0], vec_own[1], vec_own[2], vec_own[3])


def solution(mesh):
    placed = (
        P("rep", "fsdp", None),
        P("rep", None),
        P("fsdp", None),
        P("fsdp", None),
        P("fsdp", None),
        P("fsdp", None),
        P("fsdp", None),
        P("fsdp"),
        P("fsdp"),
        P("fsdp"),
        P("fsdp"),
        P("rep", "fsdp", None),
    )
    return jax.shard_map(
        shards,
        mesh=mesh,
        in_specs=placed,
        out_specs=(
            P("rep", "fsdp", None),
            P("rep", "fsdp", None),
            P("fsdp", None),
            P("fsdp", None),
            P("fsdp", None),
            P("fsdp", None),
            P("fsdp", None),
            P("fsdp"),
            P("fsdp"),
            P("fsdp"),
            P("fsdp"),
        ),
        check_vma=False,
    )
```

time: 746 us -> 300 us (0.40)
  matrix products: 251 us -> 0 us
  local copies, waits for them, and re-layouts: 172 us -> 7.13 us
  Pallas kernels: 165 us -> 276 us
  other arithmetic: 104 us -> 6.54 us
  between operations: 15 us -> 1.06 us
  starting transfers between devices: 14 us -> 3.82 us
  blocking collectives: 10.1 us -> 0 us
    dot_general x21 -> x0, matrix products: 251 us -> none  [the longest x5 45 us: product_right_t(): lax.dot_general(left_side, right_side, (((1,), (1,)), ((), ())), preferre...]
    pallas_call x1 -> x3, Pallas kernels: 165 us -> 276 us  [the longest x1 197 us: backward(): pl.pallas_call(backward_kernel, out_shape=(jax.ShapeDtypeStruct(chunks, B...]
    convert_element_type x4 -> x3, other arithmetic: 54.7 us -> 2.42 us  [the longest x1 0.91 us: shards(): key_marks = jnp.where(same | (columns >= SPLIT_LANE), 0.0, NEG).astype(BF16)]
    unnamed x112 -> x16, local copies, waits for them, and re-layouts: 51.2 us -> 5.48 us
    convert_element_type x5 -> x0, local copies, waits for them, and re-layouts: 36.7 us -> none  [the longest x4 34.6 us: row_halves(): pieces = jnp.moveaxis(pieces, 3, 1).reshape(2, -1, 384, 768).astype(BF16)]
    transpose x5 -> x0, local copies, waits for them, and re-layouts: 25.5 us -> none  [wide(): return jnp.moveaxis(summed[first:first + count], 0, 1).reshape(384, -1)]
    reduce_sum x5 -> x0, other arithmetic: 25.5 us -> none  [the longest x1 22.4 us: shards(): row_total = jnp.sum(exp_scores, axis=-1, keepdims=True)]
    slice x7 -> x0, local copies, waits for them, and re-layouts: 17.4 us -> none  [the longest x2 6.65 us: shards(): projected[:, :model_width]]
  transfers between devices with their start and end apart: 8 -> 1, of which waited for: 1 -> 0; matrix products, arithmetic and copies ran while one was open for 22% -> 2% of each run, Pallas kernels for 0% -> 21%
where the time goes in v2:
time: 300 us; the launch traced here: 294 us
  Pallas kernels  276 us (92%)
  local copies, waits for them, and re-layouts  7.13 us (2%)
  other arithmetic  6.54 us (2%)
  starting transfers between devices  3.82 us (1%)
    pallas_call x1, Pallas kernels, backward(): pl.pallas_call(backward_kernel, out_shape=(jax.ShapeDtypeStruct(chunks, B...  197 us
    pallas_call x1, Pallas kernels, forward(): pl.pallas_call(forward_kernel, out_shape=(rows, rows, rows, rows, shape(H...  61.6 us
    pallas_call x1, Pallas kernels, widen(): pl.pallas_call(widen_kernel, grid=(CHUNKS,), out_shape=(shape(1, 3), shap...  17.2 us
  transfers between devices with their start and end apart: 1, of which 0 were waited for; matrix products, arithmetic and copies ran while one was open for 2% of the time, Pallas kernels for 21%

profile of v2, /device:TPU:0, one launch (start us, length us, event | category | flops | bytes accessed | tf_op | source)
XLA Modules:
  0.0 294.4 jit_solution(11504739762872807057)
XLA Ops:
  0.6 0.0 copy-start.2
  0.7 0.0 copy-start.3
  0.7 0.0 copy-start.4
  0.7 0.0 copy-start.5
  0.7 0.0 copy-start.6
  0.7 3.8 %all-to-all-start = ((bf16[2,512,768]{2,1,0:T(8,128)(2,1)}), bf16[2,512,768]{2,1,0:T(8,128)(2,1)S(1)}, u32[]{:S(2)}, u32[]{:S(2)}) async-start(bf16[2,512,768]{2,1,0:T(8,128)(2,1)} %tokens.1), calls=%async_computation | async-start | bytes 3145728 | tf_op jit(solution)/shard_map/all_to_all | solution.py:930
  4.6 0.0 copy-done.3
  4.7 0.6 convert_element_type.19.norms
  5.3 0.2 reduce-window.4
  5.5 0.1 convert_reduce_fusion
  5.6 0.9 fusion.1.query_marks
  6.5 0.9 select_convert_fusion.key_marks
  7.4 0.1 select_reduce_fusion
  7.5 1.9 fusion.2
  9.4 1.8 pad_maximum_fusion
  11.2 61.6 %shard_map.203 = (bf16[1024,768]{1,0:T(8,128)(2,1)}, bf16[1024,768]{1,0:T(8,128)(2,1)}, bf16[1024,768]{1,0:T(8,128)(2,1)}, bf16[1024,768]{1,0:T(8,128)(2,1)}, bf...) custom-call(bf16[2,512,768]{2,1,0:T(8,128)(2,1)} %tokens.1, ...), custom_call_target="tpu_custom_call" | custom-call | tf_op jit(solution)/shard_map/pallas_call | solution.py:479
  72.9 0.0 all-to-all-done
  72.9 0.0 copy-start
  72.9 1.1 copy-done
  74.0 197.1 %shard_map.204 = (bf16[16,384,768]{2,1,0:T(8,128)(2,1)}, f32[2,512,768]{2,1,0:T(8,128)}, f32[8,768]{1,0:T(8,128)}) custom-call(bf16[1024,768]{1,0:T(8,128)(2,1)} %bitcast.10, bf16[1024,768]{1,0:T(8,128)(2,1)} %get-tuple-element.41.context, bf16[1024,768]{1,0:T(8,128)(2,1)} %get-tuple-element.42.low, bf16[1024,768]{1,0:T(8,128)(2,1)} %get-tuple-element.43.mixed, ...), custom_call_target="tpu_custom_call" | custom-call | tf_op jit(solution)/shard_map/pallas_call | solution.py:815
  271.2 17.2 %shard_map.205 = (f32[384,2304]{1,0:T(8,128)}, f32[384,768]{1,0:T(8,128)}, f32[384,3072]{1,0:T(8,128)}, f32[384,3072]{1,0:T(8,128)}, f32[1536,768]{1,0:T(8,128)}) custom-call(bf16[16,384,768]{2,1,0:T(8,128)(2,1)} %get-tuple-element.62.summed), custom_call_target="tpu_custom_call" | custom-call | tf_op jit(solution)/shard_map/pallas_call | solution.py:883
  288.3 1.6 dynamic-slice_reduce_fusion
  289.9 2.7 copy.26
  292.6 1.7 copy.27
  (17 shorter events, 0.1 us)
Async XLA Ops:
  0.6 3.9 %copy-start.2 = (bf16[384]{0:T(512)(128)(2,1)S(1)}, bf16[384]{0:T(512)(128)(2,1)}, u32[]{:S(2)}) copy-start(bf16[384]{0:T(512)(128)(2,1)} %param.19) | copy-start | bytes 2308
  0.7 3.9 %copy-start.3 = (bf16[384]{0:T(512)(128)(2,1)S(1)}, bf16[384]{0:T(512)(128)(2,1)}, u32[]{:S(2)}) copy-start(bf16[384]{0:T(512)(128)(2,1)} %param.20) | copy-start | bytes 2308
  0.7 3.9 %copy-start.4 = (bf16[384]{0:T(512)(128)(2,1)S(1)}, bf16[384]{0:T(512)(128)(2,1)}, u32[]{:S(2)}) copy-start(bf16[384]{0:T(512)(128)(2,1)} %param.21) | copy-start | bytes 2308
  0.7 3.9 %copy-start.5 = (bf16[384]{0:T(512)(128)(2,1)S(1)}, bf16[384]{0:T(512)(128)(2,1)}, u32[]{:S(2)}) copy-start(bf16[384]{0:T(512)(128)(2,1)} %param.22) | copy-start | bytes 2308
  0.7 4.6 %copy-start.6 = (s32[2,8]{1,0:T(2,128)S(1)}, s32[2,8]{1,0:T(2,128)}, u32[]{:S(2)}) copy-start(s32[2,8]{1,0:T(2,128)} %param.13) | copy-start | bytes 196
  0.7 72.2 %all-to-all-start = ((bf16[2,512,768]{2,1,0:T(8,128)(2,1)}), bf16[2,512,768]{2,1,0:T(8,128)(2,1)S(1)}, u32[]{:S(2)}, u32[]{:S(2)}) async-start(bf16[2,512,768]{2,1,0:T(8,128)(2,1)} %tokens.1), calls=%async_computation | async-start | bytes 3145728 | tf_op jit(solution)/shard_map/all_to_all | solution.py:930
  72.9 1.1 copy-start
  288.3 4.2 %copy-start.1 = (f32[2,512,768]{2,1,0:T(8,128)S(1)}, f32[2,512,768]{2,1,0:T(8,128)}, u32[]{:S(2)}) copy-start(f32[2,512,768]{2,1,0:T(8,128)} %get-tuple-element.90) | copy-start | bytes 9437188
